TPU v7x, 128 devices: a whole 4x4x4 slice. The times are simulated.
128 devices in a mesh: ctx: 32 (over z, y, x_hi), tp: 4 (over x_lo, core).
Axes of the slice: x: 4 (x_hi: 2, x_lo: 2; x = x_hi * 2 + x_lo), y: 4, z: 4, core: 2. Of those that a mesh axis runs over, the one named last changes fastest.
Arguments:
- branches: bfloat16 [3, 4096, 4096], P(None, 'ctx', 'tp'), may hold values from -6 to 6
- short_taps: float32 [3, 3, 4096], replicated, may hold values from -2.5 to 2.5
- long_filter: float32 [4096, 4096], P(('tp', 'ctx')), may hold values from 0 to 26.487934, as said below
- grad_out: bfloat16 [4096, 4096], P('ctx', 'tp'), may hold values from -6 to 6
Outputs:
- grad_branches: bfloat16 [3, 4096, 4096], P(None, 'ctx', 'tp')
- grad_filter: float32 [4096, 4096], P(('tp', 'ctx'))
Inputs may be any that keep to these rules, and one draw needn't show every extreme that they name: `long_filter`: positive filter values, applied after division by the square root of 4096.
All inputs are finite; a program needn't handle non-finite values.
Results may differ from a plain program's by a relative error of at most 0.014.
Values may be sent and summed in bfloat16 or wider, within the bound.
No kernel may reach another device: no remote copies, remote signals or barrier semaphores. Data moves between devices by JAX's collectives and lax.ppermute only.
A program may use at most 64 MiB of HBM per device.

v0:
```python
import functools

import jax
import jax.numpy as jnp
import ml_dtypes
import numpy as np
from jax import lax
from jax.experimental import pallas as pl
from jax.experimental.pallas import tpu as pltpu
from jax.sharding import PartitionSpec as P

F32 = jnp.float32
BF16 = jnp.bfloat16
CHUNK = 128
BLOCKS = 32
GROUP = 16
HALF = BLOCKS
PERIOD = 2 * BLOCKS * CHUNK
ROWS = 80
CB = 256


@functools.lru_cache(maxsize=None)
def tables():
    bf = ml_dtypes.bfloat16
    k = np.arange(HALF)[:, None] + 0.5
    m = np.arange(BLOCKS)[None, :]
    eye = np.eye(GROUP)
    phase = 2 * np.pi * k * m / (2 * BLOCKS)
    first = np.stack([np.cos(phase), -np.sin(phase)])
    lhs1 = np.einsum("qkm,st->qskmt", first, eye).reshape(2 * GROUP * HALF, BLOCKS * GROUP)
    last = np.stack([np.cos(phase), -np.sin(phase)]) * (2.0 / PERIOD)
    lhs2 = np.einsum("qkm,st->msqtk", last, eye).reshape(BLOCKS * GROUP, 2 * GROUP * HALF)
    r = np.arange(CHUNK)
    cr = 2 * np.pi * (np.outer(r, r) % CHUNK) / CHUNK
    c, s = np.cos(cr), np.sin(cr)
    fwd = np.block([[c, -s], [s, c]])
    inv = np.block([[c, s], [-s, c]])
    tw = 2 * np.pi * k * r[None, :] / PERIOD
    twist = np.stack([np.cos(tw), -np.sin(tw)]).astype(np.float32)
    return lhs1.astype(bf), lhs2.astype(bf), fwd.astype(bf), inv.astype(bf), twist


def dot(a, b):
    return jnp.dot(a, b, preferred_element_type=F32)


def head_kernel(taps_ref, br_ref, go_ref, send_ref, key_ref, val_ref):
    base = (lax.axis_index("tp") * pl.num_programs(0) + pl.program_id(0)) * CB
    cols = pl.ds(pl.multiple_of(base, CB), CB)
    row = lax.broadcasted_iota(jnp.int32, (CHUNK, CB), 0)
    row8 = lax.broadcasted_iota(jnp.int32, (8, CB), 0)
    feats, tails = [], []
    for b in range(3):
        x = br_ref[b].astype(F32)
        s0, s1, s2 = (taps_ref[b, j : j + 1, cols] for j in range(3))
        x1 = pltpu.roll(x, 1, 0)
        x2 = pltpu.roll(x, 2, 0)
        feats.append(s0 * x + s1 * jnp.where(row < 1, 0.0, x1) + s2 * jnp.where(row < 2, 0.0, x2))
        tails.append(
            jnp.where(row8 < 1, s1 * x1[:8], 0.0) + jnp.where(row8 < 2, s2 * x2[:8], 0.0)
        )
    query, key, value = feats
    go = go_ref[...].astype(F32)
    key_ref[...] = key.astype(BF16)
    val_ref[...] = value.astype(BF16)
    nd = CB // 32
    send_ref[:, 0:32, :] = (key * value).T.astype(BF16).reshape(nd, 32, CHUNK)
    send_ref[:, 32:64, :] = (go * query).T.astype(BF16).reshape(nd, 32, CHUNK)
    heads = jnp.where(
        row8 < 2,
        query[:8],
        jnp.where(
            row8 < 4,
            pltpu.roll(key[:8], 2, 0),
            jnp.where(row8 < 6, pltpu.roll(value[:8], 4, 0), pltpu.roll(go[:8], 6, 0)),
        ),
    )
    ends = jnp.where(
        row8 < 2,
        tails[0],
        jnp.where(row8 < 4, pltpu.roll(tails[1], 2, 0), pltpu.roll(tails[2], 4, 0)),
    )
    upper = lax.broadcasted_iota(jnp.int32, (8, CB), 1) // GROUP % 2 == 1
    padded = jnp.concatenate(
        [
            jnp.where(upper, 0.0, heads),
            jnp.where(upper, 0.0, ends),
            jnp.where(upper, heads, 0.0),
            jnp.where(upper, ends, 0.0),
            jnp.zeros((CHUNK - 32, CB), F32),
        ],
        axis=0,
    )
    turned = padded.T.reshape(nd, 2, GROUP, CHUNK)
    send_ref[:, 64:80, :] = (turned[:, 0] + turned[:, 1]).astype(BF16)


def twisted(real, imag, twist_ref, sign):
    shape = real.shape
    real = real.reshape(GROUP, HALF, CHUNK)
    imag = imag.reshape(GROUP, HALF, CHUNK)
    c = twist_ref[0]
    s = twist_ref[1] * sign
    out_r = (real * c - imag * s).astype(BF16).reshape(shape)
    out_i = (real * s + imag * c).astype(BF16).reshape(shape)
    return out_r, out_i


def forward(first, twist_ref, fwd_ref):
    half = GROUP * HALF
    re, im = twisted(first[:half], first[half:], twist_ref, 1.0)
    return dot(jnp.concatenate([re, im], axis=1), fwd_ref[...])


def backward(spectrum, twist_ref, inv_ref):
    value = dot(spectrum, inv_ref[...])
    re, im = twisted(value[:, :CHUNK], value[:, CHUNK:], twist_ref, -1.0)
    return jnp.concatenate([re, im], axis=0)


def filter_kernel(filter_ref, lhs1_ref, fwd_ref, twist_ref, out_ref):
    scale = (BLOCKS * CHUNK) ** -0.5
    for j in range(2):
        rows = filter_ref[GROUP * j : GROUP * (j + 1), :]
        stacked = jnp.concatenate(
            [rows[:, CHUNK * m : CHUNK * (m + 1)] for m in range(BLOCKS)], axis=0
        )
        first = dot(lhs1_ref[...], (stacked * scale).astype(BF16))
        out_ref[j] = forward(first, twist_ref, fwd_ref).astype(BF16)


def middle_kernel(
    recv_ref, spec_ref, lhs1_ref, lhs2_ref, fwd_ref, inv_ref, twist_ref, send_ref, corr_ref
):
    shape = (BLOCKS, GROUP, CHUNK)
    flat = (BLOCKS * GROUP, CHUNK)
    lane = lax.broadcasted_iota(jnp.int32, (GROUP, CHUNK), 1)
    turn = lambda x, by: pltpu.roll(x, by % CHUNK, 2)
    halo = recv_ref[:, 64:80, :].astype(F32)
    before = jnp.concatenate([jnp.zeros((1, GROUP, CHUNK), F32), halo[:-1]], axis=0)
    feat = halo + turn(before, -8)
    prod = turn(feat, -2) * turn(feat, -4)
    gate = feat * turn(halo, -6)
    spectra = []
    for at, fix in ((0, prod), (32, gate)):
        pair = []
        for j in range(2):
            x = recv_ref[:, at + GROUP * j : at + GROUP * (j + 1), :].astype(F32)
            head = fix if j == 0 else turn(fix, -GROUP)
            pair.append(jnp.where(lane < 2, head, x).astype(BF16).reshape(flat))
        first = dot(lhs1_ref[...], jnp.concatenate(pair, axis=1))
        spectra.append(
            [forward(first[:, CHUNK * j : CHUNK * (j + 1)], twist_ref, fwd_ref) for j in range(2)]
        )
    outs = []
    for j in range(2):
        pr, pi = spectra[0][j][:, :CHUNK], spectra[0][j][:, CHUNK:]
        gr, gi = spectra[1][j][:, :CHUNK], spectra[1][j][:, CHUNK:]
        hr = spec_ref[j, :, :CHUNK].astype(F32)
        hi = spec_ref[j, :, CHUNK:].astype(F32)
        join = lambda re, im: jnp.concatenate([re.astype(BF16), im.astype(BF16)], axis=1)
        corr_ref[j] = join(pr * gr + pi * gi, pr * gi - pi * gr)
        conv = backward(join(hr * pr - hi * pi, hr * pi + hi * pr), twist_ref, inv_ref)
        dzeta = backward(join(hr * gr + hi * gi, hr * gi - hi * gr), twist_ref, inv_ref)
        both = dot(lhs2_ref[...], jnp.concatenate([conv, dzeta], axis=1))
        conv = both[:, :CHUNK].reshape(shape)
        dzeta = both[:, CHUNK:].reshape(shape)
        send_ref[:, GROUP * j : GROUP * (j + 1), :] = conv.astype(BF16)
        send_ref[:, 32 + GROUP * j : 32 + GROUP * (j + 1), :] = dzeta.astype(BF16)
        outs.append((conv, dzeta))
    conv = jnp.where(lane < GROUP, outs[0][0], turn(outs[1][0], GROUP))
    dzeta = jnp.where(lane < GROUP, outs[0][1], turn(outs[1][1], GROUP))
    place = lane % GROUP
    heads = jnp.where(
        place < 2,
        conv * turn(halo, -6),
        jnp.where(place < 4, turn(dzeta, 2) * turn(feat, -2), turn(dzeta, 4) * turn(feat, 2)),
    )
    after = jnp.concatenate([heads[1:], jnp.zeros((1, GROUP, CHUNK), F32)], axis=0)
    send_ref[:, 64:80, :] = jnp.where(place < 8, feat, turn(after, 8)).astype(BF16)


def grad_filter_kernel(corr_ref, lhs2_ref, inv_ref, twist_ref, out_ref):
    scale = (BLOCKS * CHUNK) ** -0.5
    stacked = jnp.concatenate(
        [backward(corr_ref[j], twist_ref, inv_ref) for j in range(2)], axis=1
    )
    both = dot(lhs2_ref[...], stacked) * scale
    for j in range(2):
        for m in range(BLOCKS):
            out_ref[GROUP * j : GROUP * (j + 1), CHUNK * m : CHUNK * (m + 1)] = both[
                GROUP * m : GROUP * (m + 1), CHUNK * j : CHUNK * (j + 1)
            ]


def tail_kernel(taps_ref, recv_ref, key_ref, val_ref, go_ref, out_ref):
    base = (lax.axis_index("tp") * pl.num_programs(0) + pl.program_id(0)) * CB
    cols = pl.ds(pl.multiple_of(base, CB), CB)
    row8 = lax.broadcasted_iota(jnp.int32, (8, CB), 0)
    conv = recv_ref[:, 0:32, :].astype(F32).reshape(CB, CHUNK).T
    dzeta = recv_ref[:, 32:64, :].astype(F32).reshape(CB, CHUNK).T
    halo = recv_ref[:, 64:80, :].astype(F32)
    halo = jnp.concatenate([halo, pltpu.roll(halo, CHUNK - GROUP, 2)], axis=1)
    halo = halo.reshape(CB, CHUNK).T
    heads, nexts = halo[:8], halo[8:16]

    def with_head(ref, at):
        value = ref[...].astype(F32)
        first = jnp.where(row8 < 2, pltpu.roll(heads, 8 - at, 0), value[:8])
        return jnp.concatenate([first, value[8:]], axis=0)

    key = with_head(key_ref, 2)
    value = with_head(val_ref, 4)
    grads = (go_ref[...].astype(F32) * conv, dzeta * value, dzeta * key)
    for b in range(3):
        d = grads[b]
        s0, s1, s2 = (taps_ref[b, j : j + 1, cols] for j in range(3))
        d1 = pltpu.roll(d, CHUNK - 1, 0)
        d2 = pltpu.roll(d, CHUNK - 2, 0)
        e1 = jnp.where(row8 < 7, d1[-8:], pltpu.roll(nexts, (7 - 2 * b) % 8, 0))
        e2 = jnp.where(row8 < 6, d2[-8:], pltpu.roll(nexts, (6 - 2 * b) % 8, 0))
        d1 = jnp.concatenate([d1[:-8], e1], axis=0)
        d2 = jnp.concatenate([d2[:-8], e2], axis=0)
        out_ref[b] = (s0 * d + s1 * d1 + s2 * d2).astype(BF16)


def params(mib):
    return pltpu.CompilerParams(vmem_limit_bytes=mib << 20)


def exchange(x):
    return lax.all_to_all(x, "ctx", split_axis=0, concat_axis=0, tiled=True)


def per_device(branches, short_taps, long_filter, grad_out):
    sds = jax.ShapeDtypeStruct
    lhs1, lhs2, fwd, inv, twist = (jnp.asarray(t) for t in tables())
    tokens, channels = grad_out.shape
    steps = channels // CB
    nd = CB // 32
    taps_spec = pl.BlockSpec(short_taps.shape, lambda i: (0, 0, 0))
    rows_spec = pl.BlockSpec((tokens, CB), lambda i: (0, i))
    branch_spec = pl.BlockSpec((3, tokens, CB), lambda i: (0, 0, i))
    wire_spec = pl.BlockSpec((nd, ROWS, CHUNK), lambda i: (i, 0, 0))
    wire = sds((BLOCKS, ROWS, CHUNK), BF16)
    half = GROUP * HALF
    send, key, value = pl.pallas_call(
        head_kernel,
        grid=(steps,),
        in_specs=[taps_spec, branch_spec, rows_spec],
        out_specs=[wire_spec, rows_spec, rows_spec],
        out_shape=[wire, sds((tokens, channels), BF16), sds((tokens, channels), BF16)],
        compiler_params=params(16),
        name="head",
    )(short_taps, branches, grad_out)
    spectrum = pl.pallas_call(
        filter_kernel,
        out_shape=sds((2, half, 2 * CHUNK), BF16),
        compiler_params=params(32),
        name="filter_spectrum",
    )(long_filter, lhs1, fwd, twist)
    recv = exchange(send)
    back, corr = pl.pallas_call(
        middle_kernel,
        out_shape=[wire, sds((2, half, 2 * CHUNK), BF16)],
        compiler_params=params(32),
        name="middle",
    )(recv, spectrum, lhs1, lhs2, fwd, inv, twist)
    grad_filter = pl.pallas_call(
        grad_filter_kernel,
        out_shape=sds(long_filter.shape, F32),
        compiler_params=params(32),
        name="grad_filter",
    )(corr, lhs2, inv, twist)
    returned = exchange(back)
    grads = pl.pallas_call(
        tail_kernel,
        grid=(steps,),
        in_specs=[taps_spec, wire_spec, rows_spec, rows_spec, rows_spec],
        out_specs=branch_spec,
        out_shape=sds(branches.shape, BF16),
        compiler_params=params(16),
        name="tail",
    )(short_taps, returned, key, value, grad_out)
    return grads, grad_filter


def solution(mesh):
    in_specs = (P(None, "ctx", "tp"), P(), P(("tp", "ctx"), None), P("ctx", "tp"))
    out_specs = (P(None, "ctx", "tp"), P(("tp", "ctx"), None))
    return jax.shard_map(
        per_device, mesh=mesh, in_specs=in_specs, out_specs=out_specs, check_vma=False
    )
```

profile of v0, /device:TPU:0, one launch (start us, length us, event | category | flops | bytes accessed | tf_op | source)
XLA Modules:
  0.0 60.3 jit_solution(18372441792435869182)
XLA Ops:
  0.6 0.0 copy-start.1
  0.6 0.0 copy-start.2
  0.7 1.0 %copy-done.2 = bf16[128,1024]{1,0:T(8,128)(2,1)S(1)} copy-done((bf16[128,1024]{1,0:T(8,128)(2,1)S(1)}, bf16[128,1024]{1,0:T(8,128)(2,1)}, u32[]{:S(2)}) %copy-start.2) | copy-done | bytes 262168
  1.7 0.9 %copy-done.4 = f32[3,3,4096]{2,1,0:T(4,128)S(1)} copy-done((f32[3,3,4096]{2,1,0:T(4,128)S(1)}, f32[3,3,4096]{2,1,0:T(4,128)}, u32[]{:S(2)}) %copy-start.4) | copy-done | bytes 147480
  2.6 1.1 %copy-done.6 = bf16[3,128,1024]{2,1,0:T(8,128)(2,1)S(1)} copy-done((bf16[3,128,1024]{2,1,0:T(8,128)(2,1)S(1)}, bf16[3,128,1024]{2,1,0:T(8,128)(2,1)}, u32[]{:S(2)}) %copy-start.6) | copy-done | bytes 786456
  3.7 2.3 %head.1 = (bf16[32,80,128]{2,1,0:T(8,128)(2,1)}, bf16[128,1024]{1,0:T(8,128)(2,1)S(1)}, bf16[128,1024]{1,0:T(8,128)(2,1)S(1)}) custom-call(f32[3,3,4096]{2,1,0:T(4,128)S(1)} %copy-done.4, bf16[3,128,1024]{2,1,0:T(8,128)(2,1)S(1)} %copy-done.6, bf16[128,1024]{1,0:T(8,128)(2,1)S(1)} %copy-done.2), custom_call_target="tpu_custom_call" | custom-call | tf_op jit(solution)/shard_map/head/pallas_call | solution.py:248
  6.1 0.7 %copy-done.16 = bf16[128,1024]{1,0:T(8,128)(2,1)} copy-done((bf16[128,1024]{1,0:T(8,128)(2,1)}, bf16[128,1024]{1,0:T(8,128)(2,1)S(1)}, u32[]{:S(2)}) %copy-start.16) | copy-done | bytes 262168
  6.8 0.7 %copy-done.18 = bf16[128,1024]{1,0:T(8,128)(2,1)} copy-done((bf16[128,1024]{1,0:T(8,128)(2,1)}, bf16[128,1024]{1,0:T(8,128)(2,1)S(1)}, u32[]{:S(2)}) %copy-start.18) | copy-done | bytes 262168
  7.5 11.0 %all-to-all-start = ((bf16[32,80,128]{2,1,0:T(8,128)(2,1)}), bf16[32,80,128]{2,1,0:T(8,128)(2,1)S(1)}, u32[]{:S(2)}, u32[]{:S(2)}) async-start(bf16[32,80,128]{2,1,0:T(8,128)(2,1)} %get-tuple-element.7), calls=%async_computation | async-start | bytes 1310720 | tf_op jit(solution)/shard_map/all_to_all | solution.py:233
  18.5 1.0 %copy-done.10 = f32[32,4096]{1,0:T(8,128)S(1)} copy-done((f32[32,4096]{1,0:T(8,128)S(1)}, f32[32,4096]{1,0:T(8,128)}, u32[]{:S(2)}) %copy-start.10) | copy-done | bytes 524312
  19.6 0.8 %copy-done.13 = f32[2,32,128]{2,1,0:T(8,128)S(1)} copy-done((f32[2,32,128]{2,1,0:T(8,128)S(1)}, f32[2,32,128]{2,1,0:T(8,128)}, u32[]{:S(2)}) %copy-start.13) | copy-done | bytes 32792
  20.3 1.5 %filter_spectrum.1.spec_ref = bf16[2,512,256]{2,1,0:T(8,128)(2,1)S(1)} custom-call(f32[32,4096]{1,0:T(8,128)S(1)} %copy-done.10, bf16[1024,512]{1,0:T(8,128)(2,1)S(1)} %copy-done.1, bf16[256,256]{1,0:T(8,128)(2,1)S(1)} %copy-done.9, f32[2,32,128]{2,1,0:T(8,128)S(1)} %copy-done.13), custom_call_target="tpu_custom_call" | custom-call | tf_op jit(solution)/shard_map/filter_spectrum/pallas_call | solution.py:257
  21.8 11.8 %all-to-all-done.recv_ref = bf16[32,80,128]{2,1,0:T(8,128)(2,1)S(1)} async-done(((bf16[32,80,128]{2,1,0:T(8,128)(2,1)}), bf16[32,80,128]{2,1,0:T(8,128)(2,1)S(1)}, u32[]{:S(2)}, u32[]{:S(2)}) %all-to-all-start) | async-done | bytes 655392 | tf_op jit(solution)/shard_map/all_to_all | solution.py:233
  33.6 0.8 %copy-done.14 = f32[2,32,128]{2,1,0:T(8,128)S(1)} copy-done((f32[2,32,128]{2,1,0:T(8,128)S(1)}, f32[2,32,128]{2,1,0:T(8,128)}, u32[]{:S(2)}) %copy-start.14) | copy-done | bytes 32792
  34.4 3.2 %middle.1 = (bf16[32,80,128]{2,1,0:T(8,128)(2,1)S(1)}, bf16[2,512,256]{2,1,0:T(8,128)(2,1)S(1)}) custom-call(bf16[32,80,128]{2,1,0:T(8,128)(2,1)S(1)} %all-to-all-done.recv_ref, bf16[2,512,256]{2,1,0:T(8,128)(2,1)S(1)} %filter_spectrum.1.spec_ref, bf16[1024,512]{1,0:T(8,128)(2,1)S(1)} %copy-done.1, bf16[512,1024]{1,0:T(8,128)(2,1)S(1)} %copy-done, ...), custom_call_target="tpu_custom_call" | custom-call | tf_op jit(solution)/shard_map/middle/pallas_call | solution.py:264
  37.6 0.0 copy-start.7
  37.6 0.8 %copy-done.7 = bf16[32,80,128]{2,1,0:T(8,128)(2,1)} copy-done((bf16[32,80,128]{2,1,0:T(8,128)(2,1)}, bf16[32,80,128]{2,1,0:T(8,128)(2,1)S(1)}, u32[]{:S(2)}) %copy-start.7) | copy-done | bytes 655384
  38.4 0.8 %copy-done.11 = bf16[2,512,256]{2,1,0:T(8,128)(2,1)} copy-done((bf16[2,512,256]{2,1,0:T(8,128)(2,1)}, bf16[2,512,256]{2,1,0:T(8,128)(2,1)S(1)}, u32[]{:S(2)}) %copy-start.11) | copy-done | bytes 524312
  39.2 4.0 %all-to-all-start.1 = ((bf16[32,80,128]{2,1,0:T(8,128)(2,1)}), bf16[32,80,128]{2,1,0:T(8,128)(2,1)S(1)}, u32[]{:S(2)}, u32[]{:S(2)}) async-start(bf16[32,80,128]{2,1,0:T(8,128)(2,1)} %copy-done.7), calls=%async_computation.1 | async-start | bytes 1310720 | tf_op jit(solution)/shard_map/all_to_all | solution.py:233
  43.3 0.0 copy-start.5
  43.3 1.7 %grad_filter.1 = f32[32,4096]{1,0:T(8,128)} custom-call(bf16[2,512,256]{2,1,0:T(8,128)(2,1)S(1)} %copy-done.12, bf16[512,1024]{1,0:T(8,128)(2,1)S(1)} %copy-done, bf16[256,256]{1,0:T(8,128)(2,1)S(1)} %copy-done.8, f32[2,32,128]{2,1,0:T(8,128)S(1)} %copy-done.15), custom_call_target="tpu_custom_call" | custom-call | tf_op jit(solution)/shard_map/grad_filter/pallas_call | solution.py:270
  45.0 12.1 %all-to-all-done.1.recv_ref = bf16[32,80,128]{2,1,0:T(8,128)(2,1)S(1)} async-done(((bf16[32,80,128]{2,1,0:T(8,128)(2,1)}), bf16[32,80,128]{2,1,0:T(8,128)(2,1)S(1)}, u32[]{:S(2)}, u32[]{:S(2)}) %all-to-all-start.1) | async-done | bytes 655392 | tf_op jit(solution)/shard_map/all_to_all | solution.py:233
  57.2 0.9 %copy-done.19 = bf16[128,1024]{1,0:T(8,128)(2,1)S(1)} copy-done((bf16[128,1024]{1,0:T(8,128)(2,1)S(1)}, bf16[128,1024]{1,0:T(8,128)(2,1)}, u32[]{:S(2)}) %copy-start.19) | copy-done | bytes 262168
  58.1 2.2 %tail.1 = bf16[3,128,1024]{2,1,0:T(8,128)(2,1)} custom-call(f32[3,3,4096]{2,1,0:T(4,128)S(1)} %copy-done.5, bf16[32,80,128]{2,1,0:T(8,128)(2,1)S(1)} %all-to-all-done.1.recv_ref, bf16[128,1024]{1,0:T(8,128)(2,1)S(1)} %copy-done.17, bf16[128,1024]{1,0:T(8,128)(2,1)S(1)} %copy-done.19, bf16[128,1024]{1,0:T(8,128)(2,1)S(1)} %copy-done.3), custom_call_target="tpu_custom_call" | custom-call | tf_op jit(solution)/shard_map/tail/pallas_call | solution.py:277
  (25 shorter events, 0.1 us)
Async XLA Ops:
  0.6 17.9 %copy-start.1 = (bf16[1024,512]{1,0:T(8,128)(2,1)S(1)}, bf16[1024,512]{1,0:T(8,128)(2,1)}, u32[]{:S(2)}) copy-start(bf16[1024,512]{1,0:T(8,128)(2,1)} %constant.10.clone.lhs1_ref) | copy-start | bytes 3145732
  0.6 1.0 %copy-start.2 = (bf16[128,1024]{1,0:T(8,128)(2,1)S(1)}, bf16[128,1024]{1,0:T(8,128)(2,1)}, u32[]{:S(2)}) copy-start(bf16[128,1024]{1,0:T(8,128)(2,1)} %go_ref.3) | copy-start | bytes 786436
  1.7 0.9 %copy-start.4 = (f32[3,3,4096]{2,1,0:T(4,128)S(1)}, f32[3,3,4096]{2,1,0:T(4,128)}, u32[]{:S(2)}) copy-start(f32[3,3,4096]{2,1,0:T(4,128)} %taps_ref.3) | copy-start | bytes 442372
  2.6 1.1 %copy-start.6 = (bf16[3,128,1024]{2,1,0:T(8,128)(2,1)S(1)}, bf16[3,128,1024]{2,1,0:T(8,128)(2,1)}, u32[]{:S(2)}) copy-start(bf16[3,128,1024]{2,1,0:T(8,128)(2,1)} %br_ref.1) | copy-start | bytes 2359300
  6.1 0.7 %copy-start.16 = (bf16[128,1024]{1,0:T(8,128)(2,1)}, bf16[128,1024]{1,0:T(8,128)(2,1)S(1)}, u32[]{:S(2)}) copy-start(bf16[128,1024]{1,0:T(8,128)(2,1)S(1)} %get-tuple-element.9.key_ref) | copy-start | bytes 786436
  6.8 0.7 %copy-start.18 = (bf16[128,1024]{1,0:T(8,128)(2,1)}, bf16[128,1024]{1,0:T(8,128)(2,1)S(1)}, u32[]{:S(2)}) copy-start(bf16[128,1024]{1,0:T(8,128)(2,1)S(1)} %get-tuple-element.10.val_ref) | copy-start | bytes 786436
  7.5 11.0 %copy-start.9 = (bf16[256,256]{1,0:T(8,128)(2,1)S(1)}, bf16[256,256]{1,0:T(8,128)(2,1)}, u32[]{:S(2)}) copy-start(bf16[256,256]{1,0:T(8,128)(2,1)} %constant.12.clone.fwd_ref) | copy-start | bytes 393220
  7.5 26.1 %all-to-all-start = ((bf16[32,80,128]{2,1,0:T(8,128)(2,1)}), bf16[32,80,128]{2,1,0:T(8,128)(2,1)S(1)}, u32[]{:S(2)}, u32[]{:S(2)}) async-start(bf16[32,80,128]{2,1,0:T(8,128)(2,1)} %get-tuple-element.7), calls=%async_computation | async-start | bytes 1310720 | tf_op jit(solution)/shard_map/all_to_all | solution.py:233
  18.5 1.0 %copy-start.10 = (f32[32,4096]{1,0:T(8,128)S(1)}, f32[32,4096]{1,0:T(8,128)}, u32[]{:S(2)}) copy-start(f32[32,4096]{1,0:T(8,128)} %filter_ref.1) | copy-start | bytes 1572868
  19.6 0.8 %copy-start.13 = (f32[2,32,128]{2,1,0:T(8,128)S(1)}, f32[2,32,128]{2,1,0:T(8,128)}, u32[]{:S(2)}) copy-start(f32[2,32,128]{2,1,0:T(8,128)} %constant.14.clone.twist_ref) | copy-start | bytes 98308
  20.3 13.3 %copy-start = (bf16[512,1024]{1,0:T(8,128)(2,1)S(1)}, bf16[512,1024]{1,0:T(8,128)(2,1)}, u32[]{:S(2)}) copy-start(bf16[512,1024]{1,0:T(8,128)(2,1)} %constant.11.clone.lhs2_ref) | copy-start | bytes 3145732
  20.3 13.3 %copy-start.8 = (bf16[256,256]{1,0:T(8,128)(2,1)S(1)}, bf16[256,256]{1,0:T(8,128)(2,1)}, u32[]{:S(2)}) copy-start(bf16[256,256]{1,0:T(8,128)(2,1)} %constant.13.clone.inv_ref) | copy-start | bytes 393220
  33.6 0.8 %copy-start.14 = (f32[2,32,128]{2,1,0:T(8,128)S(1)}, f32[2,32,128]{2,1,0:T(8,128)}, u32[]{:S(2)}) copy-start(f32[2,32,128]{2,1,0:T(8,128)} %constant.14.clone.twist_ref) | copy-start | bytes 98308
  37.6 0.8 %copy-start.7 = (bf16[32,80,128]{2,1,0:T(8,128)(2,1)}, bf16[32,80,128]{2,1,0:T(8,128)(2,1)S(1)}, u32[]{:S(2)}) copy-start(bf16[32,80,128]{2,1,0:T(8,128)(2,1)S(1)} %get-tuple-element.8) | copy-start | bytes 1966084
  38.4 0.8 %copy-start.11 = (bf16[2,512,256]{2,1,0:T(8,128)(2,1)}, bf16[2,512,256]{2,1,0:T(8,128)(2,1)S(1)}, u32[]{:S(2)}) copy-start(bf16[2,512,256]{2,1,0:T(8,128)(2,1)S(1)} %get-tuple-element.11.corr_ref) | copy-start | bytes 1572868
  39.2 4.0 %copy-start.12 = (bf16[2,512,256]{2,1,0:T(8,128)(2,1)S(1)}, bf16[2,512,256]{2,1,0:T(8,128)(2,1)}, u32[]{:S(2)}) copy-start(bf16[2,512,256]{2,1,0:T(8,128)(2,1)} %copy-done.11) | copy-start | bytes 1572868
  39.2 4.1 %copy-start.15 = (f32[2,32,128]{2,1,0:T(8,128)S(1)}, f32[2,32,128]{2,1,0:T(8,128)}, u32[]{:S(2)}) copy-start(f32[2,32,128]{2,1,0:T(8,128)} %constant.14.clone.twist_ref) | copy-start | bytes 98308
  39.2 18.0 %all-to-all-start.1 = ((bf16[32,80,128]{2,1,0:T(8,128)(2,1)}), bf16[32,80,128]{2,1,0:T(8,128)(2,1)S(1)}, u32[]{:S(2)}, u32[]{:S(2)}) async-start(bf16[32,80,128]{2,1,0:T(8,128)(2,1)} %copy-done.7), calls=%async_computation.1 | async-start | bytes 1310720 | tf_op jit(solution)/shard_map/all_to_all | solution.py:233
  43.3 13.9 %copy-start.3 = (bf16[128,1024]{1,0:T(8,128)(2,1)S(1)}, bf16[128,1024]{1,0:T(8,128)(2,1)}, u32[]{:S(2)}) copy-start(bf16[128,1024]{1,0:T(8,128)(2,1)} %go_ref.3) | copy-start | bytes 786436
  43.3 13.9 %copy-start.5 = (f32[3,3,4096]{2,1,0:T(4,128)S(1)}, f32[3,3,4096]{2,1,0:T(4,128)}, u32[]{:S(2)}) copy-start(f32[3,3,4096]{2,1,0:T(4,128)} %taps_ref.3) | copy-start | bytes 442372
  43.3 13.9 %copy-start.17 = (bf16[128,1024]{1,0:T(8,128)(2,1)S(1)}, bf16[128,1024]{1,0:T(8,128)(2,1)}, u32[]{:S(2)}) copy-start(bf16[128,1024]{1,0:T(8,128)(2,1)} %copy-done.16) | copy-start | bytes 786436
  57.2 1.0 %copy-start.19 = (bf16[128,1024]{1,0:T(8,128)(2,1)S(1)}, bf16[128,1024]{1,0:T(8,128)(2,1)}, u32[]{:S(2)}) copy-start(bf16[128,1024]{1,0:T(8,128)(2,1)} %copy-done.18) | copy-start | bytes 786436
where the time goes:
time: 60.9 us; the launch traced here: 60.3 us
  waiting for transfers between devices  23.9 us (39%)
  starting transfers between devices  15 us (25%)
  Pallas kernels  10.9 us (18%)
  local copies, waits for them, and re-layouts  9.66 us (16%)
  between operations  0.77 us (1%)
    all_to_all x2, waiting for transfers between devices, exchange(): return lax.all_to_all(x, 'ctx', split_axis=0, concat_axis=0, tiled=True)  23.9 us
    all_to_all x2, starting transfers between devices, exchange(): return lax.all_to_all(x, 'ctx', split_axis=0, concat_axis=0, tiled=True)  15 us
    unnamed x40, local copies, waits for them, and re-layouts  9.66 us
    pallas_call x1, Pallas kernels, per_device(): pl.pallas_call(middle_kernel, out_shape=[wire, sds((2, half, 2 * CHUNK),...  3.17 us
    pallas_call x1, Pallas kernels, per_device(): pl.pallas_call(head_kernel, grid=(steps,), in_specs=[taps_spec, branch_sp...  2.33 us
    pallas_call x1, Pallas kernels, per_device(): pl.pallas_call(tail_kernel, grid=(steps,), in_specs=[taps_spec, wire_spec...  2.19 us
    pallas_call x1, Pallas kernels, per_device(): pl.pallas_call(grad_filter_kernel, out_shape=sds(long_filter.shape, F32),...  1.75 us
    pallas_call x1, Pallas kernels, per_device(): pl.pallas_call(filter_kernel, out_shape=sds((2, half, 2 * CHUNK), BF16),...  1.47 us
  transfers between devices with their start and end apart: 2, of which 2 were waited for; matrix products, arithmetic and copies ran while one was open for 0% of the time, Pallas kernels for 5%

commit v1 on v0

--- a/solution.py
+++ b/solution.py
@@ -45,28 +45,37 @@
     return jnp.dot(a, b, preferred_element_type=F32)
 
 
-def head_kernel(taps_ref, br_ref, go_ref, send_ref, key_ref, val_ref):
-    base = (lax.axis_index("tp") * pl.num_programs(0) + pl.program_id(0)) * CB
-    cols = pl.ds(pl.multiple_of(base, CB), CB)
-    row = lax.broadcasted_iota(jnp.int32, (CHUNK, CB), 0)
+def taps_slice(taps_ref, channels):
+    return taps_ref.at[:, :, pl.ds(pl.multiple_of(lax.axis_index("tp") * channels, 128), channels)]
+
+
+def featurize(x, taps):
+    row = lax.broadcasted_iota(jnp.int32, x.shape, 0)
+    s0, s1, s2 = taps
+    x1 = pltpu.roll(x, 1, 0)
+    x2 = pltpu.roll(x, 2, 0)
+    feat = s0 * x + s1 * jnp.where(row < 1, 0.0, x1) + s2 * jnp.where(row < 2, 0.0, x2)
+    row = row[:8]
+    tail = jnp.where(row < 1, s1 * x1[:8], 0.0) + jnp.where(row < 2, s2 * x2[:8], 0.0)
+    return feat, tail
+
+
+def head_block(taps_ref, br_ref, go_ref, send_ref, at):
+    cols = pl.ds(at, CB)
+    nd = CB // 32
+    out = pl.ds(at // 32, nd)
     row8 = lax.broadcasted_iota(jnp.int32, (8, CB), 0)
     feats, tails = [], []
     for b in range(3):
-        x = br_ref[b].astype(F32)
-        s0, s1, s2 = (taps_ref[b, j : j + 1, cols] for j in range(3))
-        x1 = pltpu.roll(x, 1, 0)
-        x2 = pltpu.roll(x, 2, 0)
-        feats.append(s0 * x + s1 * jnp.where(row < 1, 0.0, x1) + s2 * jnp.where(row < 2, 0.0, x2))
-        tails.append(
-            jnp.where(row8 < 1, s1 * x1[:8], 0.0) + jnp.where(row8 < 2, s2 * x2[:8], 0.0)
+        feat, tail = featurize(
+            br_ref[b, :, cols].astype(F32), [taps_ref[b, j : j + 1, cols] for j in range(3)]
         )
+        feats.append(feat)
+        tails.append(tail)
     query, key, value = feats
-    go = go_ref[...].astype(F32)
-    key_ref[...] = key.astype(BF16)
-    val_ref[...] = value.astype(BF16)
-    nd = CB // 32
-    send_ref[:, 0:32, :] = (key * value).T.astype(BF16).reshape(nd, 32, CHUNK)
-    send_ref[:, 32:64, :] = (go * query).T.astype(BF16).reshape(nd, 32, CHUNK)
+    go = go_ref[:, cols].astype(F32)
+    send_ref[out, 0:32, :] = (key * value).T.astype(BF16).reshape(nd, 32, CHUNK)
+    send_ref[out, 32:64, :] = (go * query).T.astype(BF16).reshape(nd, 32, CHUNK)
     heads = jnp.where(
         row8 < 2,
         query[:8],
@@ -93,7 +102,39 @@
         axis=0,
     )
     turned = padded.T.reshape(nd, 2, GROUP, CHUNK)
-    send_ref[:, 64:80, :] = (turned[:, 0] + turned[:, 1]).astype(BF16)
+    send_ref[out, 64:80, :] = (turned[:, 0] + turned[:, 1]).astype(BF16)
+
+
+def head_kernel(
+    taps_hbm, br_hbm, go_hbm, send_hbm, taps_ref, br_ref, go_ref, send_ref, taps_sem, in_sem, out_sem
+):
+    channels = go_ref.shape[1]
+    nd = CB // 32
+    taps_copy = pltpu.make_async_copy(taps_slice(taps_hbm, channels), taps_ref, taps_sem)
+    taps_copy.start()
+    loads, stores = [], []
+    for i in range(channels // CB):
+        cols = pl.ds(i * CB, CB)
+        loads.append(
+            [
+                pltpu.make_async_copy(
+                    br_hbm.at[:, :, cols], br_ref.at[:, :, cols], in_sem.at[0, i]
+                ),
+                pltpu.make_async_copy(go_hbm.at[:, cols], go_ref.at[:, cols], in_sem.at[1, i]),
+            ]
+        )
+        for copy in loads[-1]:
+            copy.start()
+    taps_copy.wait()
+    for i in range(channels // CB):
+        for copy in loads[i]:
+            copy.wait()
+        head_block(taps_ref, br_ref, go_ref, send_ref, i * CB)
+        out = pl.ds(i * nd, nd)
+        stores.append(pltpu.make_async_copy(send_ref.at[out], send_hbm.at[out], out_sem.at[i]))
+        stores[-1].start()
+    for copy in stores:
+        copy.wait()
 
 
 def twisted(real, imag, twist_ref, sign):
@@ -131,8 +172,22 @@
 
 
 def middle_kernel(
-    recv_ref, spec_ref, lhs1_ref, lhs2_ref, fwd_ref, inv_ref, twist_ref, send_ref, corr_ref
+    recv_ref,
+    spec_ref,
+    lhs1_ref,
+    lhs2_hbm,
+    fwd_ref,
+    inv_ref,
+    twist_ref,
+    send_hbm,
+    corr_ref,
+    lhs2_ref,
+    send_ref,
+    lhs2_sem,
+    out_sem,
 ):
+    lhs2_copy = pltpu.make_async_copy(lhs2_hbm, lhs2_ref, lhs2_sem)
+    lhs2_copy.start()
     shape = (BLOCKS, GROUP, CHUNK)
     flat = (BLOCKS * GROUP, CHUNK)
     lane = lax.broadcasted_iota(jnp.int32, (GROUP, CHUNK), 1)
@@ -163,6 +218,8 @@
         corr_ref[j] = join(pr * gr + pi * gi, pr * gi - pi * gr)
         conv = backward(join(hr * pr - hi * pi, hr * pi + hi * pr), twist_ref, inv_ref)
         dzeta = backward(join(hr * gr + hi * gi, hr * gi - hi * gr), twist_ref, inv_ref)
+        if j == 0:
+            lhs2_copy.wait()
         both = dot(lhs2_ref[...], jnp.concatenate([conv, dzeta], axis=1))
         conv = both[:, :CHUNK].reshape(shape)
         dzeta = both[:, CHUNK:].reshape(shape)
@@ -179,9 +236,42 @@
     )
     after = jnp.concatenate([heads[1:], jnp.zeros((1, GROUP, CHUNK), F32)], axis=0)
     send_ref[:, 64:80, :] = jnp.where(place < 8, feat, turn(after, 8)).astype(BF16)
-
-
-def grad_filter_kernel(corr_ref, lhs2_ref, inv_ref, twist_ref, out_ref):
+    out = pltpu.make_async_copy(send_ref, send_hbm, out_sem)
+    out.start()
+    out.wait()
+
+
+def grad_filter_kernel(
+    taps_hbm,
+    br_hbm,
+    go_hbm,
+    corr_ref,
+    lhs2_hbm,
+    inv_ref,
+    twist_ref,
+    out_ref,
+    taps_ref,
+    rows_ref,
+    lhs2_ref,
+    br_ref,
+    sems,
+):
+    channels = go_hbm.shape[1]
+    copies = [
+        pltpu.make_async_copy(lhs2_hbm, lhs2_ref, sems.at[0]),
+        pltpu.make_async_copy(taps_slice(taps_hbm, channels), taps_ref, sems.at[1]),
+        pltpu.make_async_copy(br_hbm.at[1:3], br_ref, sems.at[2]),
+        pltpu.make_async_copy(go_hbm, rows_ref.at[2], sems.at[3]),
+    ]
+    for copy in copies:
+        copy.start()
+    for copy in copies:
+        copy.wait()
+    for i in range(channels // CB):
+        cols = pl.ds(i * CB, CB)
+        for b in range(2):
+            taps = [taps_ref[b + 1, j : j + 1, cols] for j in range(3)]
+            rows_ref[b, :, cols] = featurize(br_ref[b, :, cols].astype(F32), taps)[0].astype(BF16)
     scale = (BLOCKS * CHUNK) ** -0.5
     stacked = jnp.concatenate(
         [backward(corr_ref[j], twist_ref, inv_ref) for j in range(2)], axis=1
@@ -194,25 +284,25 @@
             ]
 
 
-def tail_kernel(taps_ref, recv_ref, key_ref, val_ref, go_ref, out_ref):
-    base = (lax.axis_index("tp") * pl.num_programs(0) + pl.program_id(0)) * CB
-    cols = pl.ds(pl.multiple_of(base, CB), CB)
+def tail_block(taps_ref, rows_ref, recv_ref, out_ref, at):
+    cols = pl.ds(at, CB)
+    src = pl.ds(at // 32, CB // 32)
     row8 = lax.broadcasted_iota(jnp.int32, (8, CB), 0)
-    conv = recv_ref[:, 0:32, :].astype(F32).reshape(CB, CHUNK).T
-    dzeta = recv_ref[:, 32:64, :].astype(F32).reshape(CB, CHUNK).T
-    halo = recv_ref[:, 64:80, :].astype(F32)
+    conv = recv_ref[src, 0:32, :].astype(F32).reshape(CB, CHUNK).T
+    dzeta = recv_ref[src, 32:64, :].astype(F32).reshape(CB, CHUNK).T
+    halo = recv_ref[src, 64:80, :].astype(F32)
     halo = jnp.concatenate([halo, pltpu.roll(halo, CHUNK - GROUP, 2)], axis=1)
     halo = halo.reshape(CB, CHUNK).T
     heads, nexts = halo[:8], halo[8:16]
 
-    def with_head(ref, at):
-        value = ref[...].astype(F32)
+    def with_head(b, at):
+        value = rows_ref[b, :, cols].astype(F32)
         first = jnp.where(row8 < 2, pltpu.roll(heads, 8 - at, 0), value[:8])
         return jnp.concatenate([first, value[8:]], axis=0)
 
-    key = with_head(key_ref, 2)
-    value = with_head(val_ref, 4)
-    grads = (go_ref[...].astype(F32) * conv, dzeta * value, dzeta * key)
+    key = with_head(0, 2)
+    value = with_head(1, 4)
+    grads = (rows_ref[2, :, cols].astype(F32) * conv, dzeta * value, dzeta * key)
     for b in range(3):
         d = grads[b]
         s0, s1, s2 = (taps_ref[b, j : j + 1, cols] for j in range(3))
@@ -222,7 +312,20 @@
         e2 = jnp.where(row8 < 6, d2[-8:], pltpu.roll(nexts, (6 - 2 * b) % 8, 0))
         d1 = jnp.concatenate([d1[:-8], e1], axis=0)
         d2 = jnp.concatenate([d2[:-8], e2], axis=0)
-        out_ref[b] = (s0 * d + s1 * d1 + s2 * d2).astype(BF16)
+        out_ref[b, :, cols] = (s0 * d + s1 * d1 + s2 * d2).astype(BF16)
+
+
+def tail_kernel(taps_ref, rows_ref, recv_ref, out_hbm, out_ref, sem):
+    stores = []
+    for i in range(out_ref.shape[2] // CB):
+        tail_block(taps_ref, rows_ref, recv_ref, out_ref, i * CB)
+        cols = pl.ds(i * CB, CB)
+        stores.append(
+            pltpu.make_async_copy(out_ref.at[:, :, cols], out_hbm.at[:, :, cols], sem.at[i])
+        )
+        stores[-1].start()
+    for copy in stores:
+        copy.wait()
 
 
 def params(mib):
@@ -234,55 +337,79 @@
 
 
 def per_device(branches, short_taps, long_filter, grad_out):
-    sds = jax.ShapeDtypeStruct
     lhs1, lhs2, fwd, inv, twist = (jnp.asarray(t) for t in tables())
     tokens, channels = grad_out.shape
     steps = channels // CB
-    nd = CB // 32
-    taps_spec = pl.BlockSpec(short_taps.shape, lambda i: (0, 0, 0))
-    rows_spec = pl.BlockSpec((tokens, CB), lambda i: (0, i))
-    branch_spec = pl.BlockSpec((3, tokens, CB), lambda i: (0, 0, i))
-    wire_spec = pl.BlockSpec((nd, ROWS, CHUNK), lambda i: (i, 0, 0))
-    wire = sds((BLOCKS, ROWS, CHUNK), BF16)
     half = GROUP * HALF
-    send, key, value = pl.pallas_call(
+    hbm = pl.BlockSpec(memory_space=pltpu.HBM)
+    vmem = pl.BlockSpec(memory_space=pltpu.VMEM)
+    dma = pltpu.SemaphoreType.DMA
+    wire = (BLOCKS, ROWS, CHUNK)
+    spectral = (2, half, 2 * CHUNK)
+    held = lambda x: pltpu.with_memory_space_constraint(x, pltpu.HBM)
+    branches, short_taps, grad_out, lhs2 = map(held, (branches, short_taps, grad_out, lhs2))
+    send = pl.pallas_call(
         head_kernel,
-        grid=(steps,),
-        in_specs=[taps_spec, branch_spec, rows_spec],
-        out_specs=[wire_spec, rows_spec, rows_spec],
-        out_shape=[wire, sds((tokens, channels), BF16), sds((tokens, channels), BF16)],
-        compiler_params=params(16),
+        in_specs=[hbm, hbm, hbm],
+        out_specs=hbm,
+        out_shape=pltpu.HBM(wire, BF16),
+        scratch_shapes=[
+            pltpu.VMEM((3, 3, channels), F32),
+            pltpu.VMEM((3, tokens, channels), BF16),
+            pltpu.VMEM((tokens, channels), BF16),
+            pltpu.VMEM(wire, BF16),
+            dma,
+            dma((2, steps)),
+            dma((steps,)),
+        ],
+        compiler_params=params(24),
         name="head",
     )(short_taps, branches, grad_out)
     spectrum = pl.pallas_call(
         filter_kernel,
-        out_shape=sds((2, half, 2 * CHUNK), BF16),
+        in_specs=[vmem] * 4,
+        out_specs=vmem,
+        out_shape=pltpu.VMEM(spectral, BF16),
         compiler_params=params(32),
         name="filter_spectrum",
     )(long_filter, lhs1, fwd, twist)
     recv = exchange(send)
     back, corr = pl.pallas_call(
         middle_kernel,
-        out_shape=[wire, sds((2, half, 2 * CHUNK), BF16)],
+        in_specs=[vmem, vmem, vmem, hbm, vmem, vmem, vmem],
+        out_specs=[hbm, vmem],
+        out_shape=[pltpu.HBM(wire, BF16), pltpu.VMEM(spectral, BF16)],
+        scratch_shapes=[pltpu.VMEM(lhs2.shape, BF16), pltpu.VMEM(wire, BF16), dma, dma],
         compiler_params=params(32),
         name="middle",
     )(recv, spectrum, lhs1, lhs2, fwd, inv, twist)
-    grad_filter = pl.pallas_call(
+    grad_filter, taps, rows = pl.pallas_call(
         grad_filter_kernel,
-        out_shape=sds(long_filter.shape, F32),
+        in_specs=[hbm, hbm, hbm, vmem, hbm, vmem, vmem],
+        out_specs=[vmem, vmem, vmem],
+        out_shape=[
+            jax.ShapeDtypeStruct(long_filter.shape, F32),
+            pltpu.VMEM((3, 3, channels), F32),
+            pltpu.VMEM((3, tokens, channels), BF16),
+        ],
+        scratch_shapes=[
+            pltpu.VMEM(lhs2.shape, BF16),
+            pltpu.VMEM((2, tokens, channels), BF16),
+            dma((4,)),
+        ],
         compiler_params=params(32),
         name="grad_filter",
-    )(corr, lhs2, inv, twist)
+    )(short_taps, branches, grad_out, corr, lhs2, inv, twist)
     returned = exchange(back)
     grads = pl.pallas_call(
         tail_kernel,
-        grid=(steps,),
-        in_specs=[taps_spec, wire_spec, rows_spec, rows_spec, rows_spec],
-        out_specs=branch_spec,
-        out_shape=sds(branches.shape, BF16),
-        compiler_params=params(16),
+        in_specs=[vmem, vmem, vmem],
+        out_specs=hbm,
+        out_shape=pltpu.HBM(branches.shape, BF16),
+        scratch_shapes=[pltpu.VMEM(branches.shape, BF16), dma((steps,))],
+        compiler_params=params(24),
         name="tail",
-    )(short_taps, returned, key, value, grad_out)
+    )(taps, rows, returned)
     return grads, grad_filter
 
 

time: 60.9 us -> 54.1 us (0.89)
  local copies, waits for them, and re-layouts: 9.66 us -> 0.03 us
  Pallas kernels: 10.9 us -> 14 us
    unnamed x40 -> x10, local copies, waits for them, and re-layouts: 9.66 us -> 0.03 us
    pallas_call x5, Pallas kernels: 10.9 us -> 14 us  [the longest x1 4.31 us: per_device(): pl.pallas_call(middle_kernel, in_specs=[vmem, vmem, vmem, hbm, vmem, vmem...]
  transfers between devices with their start and end apart: 2 -> 2, of which waited for: 2 -> 2; matrix products, arithmetic and copies ran while one was open for 0% -> 0% of each run, Pallas kernels for 5% -> 9%
where the time goes in v1:
time: 54.1 us; the launch traced here: 53.7 us
  waiting for transfers between devices  24 us (44%)
  starting transfers between devices  14.9 us (28%)
  Pallas kernels  14 us (26%)
  between operations  0.75 us (1%)
    all_to_all x2, waiting for transfers between devices, exchange(): return lax.all_to_all(x, 'ctx', split_axis=0, concat_axis=0, tiled=True)  24 us
    all_to_all x2, starting transfers between devices, exchange(): return lax.all_to_all(x, 'ctx', split_axis=0, concat_axis=0, tiled=True)  14.9 us
    pallas_call x1, Pallas kernels, per_device(): pl.pallas_call(middle_kernel, in_specs=[vmem, vmem, vmem, hbm, vmem, vmem...  4.31 us
    pallas_call x1, Pallas kernels, per_device(): pl.pallas_call(grad_filter_kernel, in_specs=[hbm, hbm, hbm, vmem, hbm, vm...  3.48 us
    pallas_call x1, Pallas kernels, per_device(): pl.pallas_call(head_kernel, in_specs=[hbm, hbm, hbm], out_specs=hbm, out_...  3.19 us
    pallas_call x1, Pallas kernels, per_device(): pl.pallas_call(tail_kernel, in_specs=[vmem, vmem, vmem], out_specs=hbm, o...  1.56 us
    pallas_call x1, Pallas kernels, per_device(): pl.pallas_call(filter_kernel, in_specs=[vmem] * 4, out_specs=vmem, out_sh...  1.48 us
  transfers between devices with their start and end apart: 2, of which 2 were waited for; matrix products, arithmetic and copies ran while one was open for 0% of the time, Pallas kernels for 9%

profile of v1, /device:TPU:0, one launch (start us, length us, event | category | flops | bytes accessed | tf_op | source)
XLA Modules:
  0.0 53.7 jit_solution(1778669559266637670)
XLA Ops:
  0.6 0.0 copy-start.3
  0.6 3.2 %head.1 = bf16[32,80,128]{2,1,0:T(8,128)(2,1)} custom-call(f32[3,3,4096]{2,1,0:T(4,128)} %taps_hbm.3, bf16[3,128,1024]{2,1,0:T(8,128)(2,1)} %br_hbm.3, bf16[128,1024]{1,0:T(8,128)(2,1)} %go_hbm.3), custom_call_target="tpu_custom_call" | custom-call | tf_op jit(solution)/shard_map/head/pallas_call | solution.py:351
  3.8 0.0 copy-start
  3.8 0.0 copy-start.2
  3.9 0.0 copy-start.4
  3.9 11.0 %all-to-all-start = ((bf16[32,80,128]{2,1,0:T(8,128)(2,1)}), bf16[32,80,128]{2,1,0:T(8,128)(2,1)S(1)}, u32[]{:S(2)}, u32[]{:S(2)}) async-start(bf16[32,80,128]{2,1,0:T(8,128)(2,1)} %head.1), calls=%async_computation | async-start | bytes 1310720 | tf_op jit(solution)/shard_map/all_to_all | solution.py:336
  14.9 0.0 copy-done.3
  14.9 0.0 copy-done
  14.9 0.0 copy-done.2
  14.9 0.0 copy-done.4
  14.9 0.0 copy-start.1
  15.0 1.5 %filter_spectrum.1.spec_ref = bf16[2,512,256]{2,1,0:T(8,128)(2,1)S(1)} custom-call(f32[32,4096]{1,0:T(8,128)S(1)} %copy-done.3, bf16[1024,512]{1,0:T(8,128)(2,1)S(1)} %copy-done, bf16[256,256]{1,0:T(8,128)(2,1)S(1)} %copy-done.2, f32[2,32,128]{2,1,0:T(8,128)S(1)} %copy-done.4), custom_call_target="tpu_custom_call" | custom-call | tf_op jit(solution)/shard_map/filter_spectrum/pallas_call | solution.py:368
  16.4 13.6 %all-to-all-done.recv_ref = bf16[32,80,128]{2,1,0:T(8,128)(2,1)S(1)} async-done(((bf16[32,80,128]{2,1,0:T(8,128)(2,1)}), bf16[32,80,128]{2,1,0:T(8,128)(2,1)S(1)}, u32[]{:S(2)}, u32[]{:S(2)}) %all-to-all-start) | async-done | bytes 655392 | tf_op jit(solution)/shard_map/all_to_all | solution.py:336
  30.0 0.0 copy-done.1
  30.0 4.3 %middle.1 = (bf16[32,80,128]{2,1,0:T(8,128)(2,1)}, bf16[2,512,256]{2,1,0:T(8,128)(2,1)S(1)}) custom-call(bf16[32,80,128]{2,1,0:T(8,128)(2,1)S(1)} %all-to-all-done.recv_ref, bf16[2,512,256]{2,1,0:T(8,128)(2,1)S(1)} %filter_spectrum.1.spec_ref, bf16[1024,512]{1,0:T(8,128)(2,1)S(1)} %copy-done, bf16[512,1024]{1,0:T(8,128)(2,1)} %constant.11.clone.lhs2_hbm, ...), custom_call_target="tpu_custom_call" | custom-call | tf_op jit(solution)/shard_map/middle/pallas_call | solution.py:377
  34.3 3.9 %all-to-all-start.1 = ((bf16[32,80,128]{2,1,0:T(8,128)(2,1)}), bf16[32,80,128]{2,1,0:T(8,128)(2,1)S(1)}, u32[]{:S(2)}, u32[]{:S(2)}) async-start(bf16[32,80,128]{2,1,0:T(8,128)(2,1)} %get-tuple-element.10), calls=%async_computation.1 | async-start | bytes 1310720 | tf_op jit(solution)/shard_map/all_to_all | solution.py:336
  38.3 3.5 %grad_filter.1 = (f32[32,4096]{1,0:T(8,128)}, f32[3,3,1024]{2,1,0:T(4,128)S(1)}, bf16[3,128,1024]{2,1,0:T(8,128)(2,1)S(1)}) custom-call(f32[3,3,4096]{2,1,0:T(4,128)} %taps_hbm.3, bf16[3,128,1024]{2,1,0:T(8,128)(2,1)} %br_hbm.3, bf16[128,1024]{1,0:T(8,128)(2,1)} %go_hbm.3, bf16[2,512,256]{2,1,0:T(8,128)(2,1)S(1)} %get-tuple-element.7.corr_ref, ...), custom_call_target="tpu_custom_call" | custom-call | tf_op jit(solution)/shard_map/grad_filter/pallas_call | solution.py:386
  41.8 10.4 %all-to-all-done.1.recv_ref = bf16[32,80,128]{2,1,0:T(8,128)(2,1)S(1)} async-done(((bf16[32,80,128]{2,1,0:T(8,128)(2,1)}), bf16[32,80,128]{2,1,0:T(8,128)(2,1)S(1)}, u32[]{:S(2)}, u32[]{:S(2)}) %all-to-all-start.1) | async-done | bytes 655392 | tf_op jit(solution)/shard_map/all_to_all | solution.py:336
  52.2 1.6 %tail.1 = bf16[3,128,1024]{2,1,0:T(8,128)(2,1)} custom-call(f32[3,3,1024]{2,1,0:T(4,128)S(1)} %get-tuple-element.8.taps_ref, bf16[3,128,1024]{2,1,0:T(8,128)(2,1)S(1)} %get-tuple-element.9.rows_ref, bf16[32,80,128]{2,1,0:T(8,128)(2,1)S(1)} %all-to-all-done.1.recv_ref), custom_call_target="tpu_custom_call" | custom-call | tf_op jit(solution)/shard_map/tail/pallas_call | solution.py:404
Async XLA Ops:
  0.6 14.3 %copy-start.3 = (f32[32,4096]{1,0:T(8,128)S(1)}, f32[32,4096]{1,0:T(8,128)}, u32[]{:S(2)}) copy-start(f32[32,4096]{1,0:T(8,128)} %filter_ref.1) | copy-start | bytes 1572868
  3.8 11.1 %copy-start = (bf16[1024,512]{1,0:T(8,128)(2,1)S(1)}, bf16[1024,512]{1,0:T(8,128)(2,1)}, u32[]{:S(2)}) copy-start(bf16[1024,512]{1,0:T(8,128)(2,1)} %constant.10.clone.lhs1_ref) | copy-start | bytes 3145732
  3.8 11.1 %copy-start.2 = (bf16[256,256]{1,0:T(8,128)(2,1)S(1)}, bf16[256,256]{1,0:T(8,128)(2,1)}, u32[]{:S(2)}) copy-start(bf16[256,256]{1,0:T(8,128)(2,1)} %constant.12.clone.fwd_ref) | copy-start | bytes 393220
  3.9 11.1 %copy-start.4 = (f32[2,32,128]{2,1,0:T(8,128)S(1)}, f32[2,32,128]{2,1,0:T(8,128)}, u32[]{:S(2)}) copy-start(f32[2,32,128]{2,1,0:T(8,128)} %constant.14.clone.twist_ref) | copy-start | bytes 98308
  3.9 26.2 %all-to-all-start = ((bf16[32,80,128]{2,1,0:T(8,128)(2,1)}), bf16[32,80,128]{2,1,0:T(8,128)(2,1)S(1)}, u32[]{:S(2)}, u32[]{:S(2)}) async-start(bf16[32,80,128]{2,1,0:T(8,128)(2,1)} %head.1), calls=%async_computation | async-start | bytes 1310720 | tf_op jit(solution)/shard_map/all_to_all | solution.py:336
  14.9 15.1 %copy-start.1 = (bf16[256,256]{1,0:T(8,128)(2,1)S(1)}, bf16[256,256]{1,0:T(8,128)(2,1)}, u32[]{:S(2)}) copy-start(bf16[256,256]{1,0:T(8,128)(2,1)} %constant.13.clone.inv_ref) | copy-start | bytes 393220
  34.3 17.8 %all-to-all-start.1 = ((bf16[32,80,128]{2,1,0:T(8,128)(2,1)}), bf16[32,80,128]{2,1,0:T(8,128)(2,1)S(1)}, u32[]{:S(2)}, u32[]{:S(2)}) async-start(bf16[32,80,128]{2,1,0:T(8,128)(2,1)} %get-tuple-element.10), calls=%async_computation.1 | async-start | bytes 1310720 | tf_op jit(solution)/shard_map/all_to_all | solution.py:336

commit v2 on v1

v2 whole, which is shorter than its diff:
```python
import functools

import jax
import jax.numpy as jnp
import ml_dtypes
import numpy as np
from jax import lax
from jax.experimental import pallas as pl
from jax.experimental.pallas import tpu as pltpu
from jax.sharding import PartitionSpec as P

F32 = jnp.float32
BF16 = jnp.bfloat16
CHUNK = 128
BLOCKS = 32
GROUP = 8
SPAN = 8
SLOT = 16
HALF = BLOCKS
PERIOD = 2 * BLOCKS * CHUNK
ROWS = 72
CB = 256

ORDER_IN = [i ^ 21 for i in range(BLOCKS)]
ORDER_OUT = [i ^ 21 for i in range(BLOCKS)]
PLACE_IN = [ORDER_IN.index(i) for i in range(BLOCKS)]
PLACE_OUT = [ORDER_OUT.index(i) for i in range(BLOCKS)]


@functools.lru_cache(maxsize=None)
def tables():
    bf = ml_dtypes.bfloat16
    k = np.arange(HALF)[:, None] + 0.5
    m = np.arange(BLOCKS)[None, :]
    eye = np.eye(GROUP)
    phase = 2 * np.pi * k * m / (2 * BLOCKS)
    first = np.stack([np.cos(phase), -np.sin(phase)])
    lhs1 = np.einsum("qkm,st->sqkmt", first[:, :, ORDER_IN], eye).reshape(2 * GROUP * HALF, BLOCKS * GROUP)
    last = np.stack([np.cos(phase), -np.sin(phase)]) * (2.0 / PERIOD)
    lhs2 = np.einsum("qkm,st->mstqk", last[:, :, ORDER_OUT], eye).reshape(BLOCKS * GROUP, 2 * GROUP * HALF)
    r = np.arange(CHUNK)
    cr = 2 * np.pi * (np.outer(r, r) % CHUNK) / CHUNK
    c, s = np.cos(cr), np.sin(cr)
    fwd = np.block([[c, -s], [s, c]])
    inv = np.block([[c, s], [-s, c]])
    tw = 2 * np.pi * k * r[None, :] / PERIOD
    twist = np.stack([np.cos(tw), -np.sin(tw)]).astype(np.float32)
    return lhs1.astype(bf), lhs2.astype(bf), fwd.astype(bf), inv.astype(bf), twist


def take(x, order):
    return jnp.concatenate([x[i : i + 1] for i in order], axis=0)


def dot(a, b):
    return jnp.dot(a, b, preferred_element_type=F32)


def taps_slice(taps_ref, channels):
    return taps_ref.at[:, :, pl.ds(pl.multiple_of(lax.axis_index("tp") * channels, 128), channels)]


def featurize(x, taps):
    row = lax.broadcasted_iota(jnp.int32, x.shape, 0)
    s0, s1, s2 = taps
    x1 = pltpu.roll(x, 1, 0)
    x2 = pltpu.roll(x, 2, 0)
    feat = s0 * x + s1 * jnp.where(row < 1, 0.0, x1) + s2 * jnp.where(row < 2, 0.0, x2)
    row = row[:8]
    tail = jnp.where(row < 1, s1 * x1[:8], 0.0) + jnp.where(row < 2, s2 * x2[:8], 0.0)
    return feat, tail


def head_block(taps_ref, br_ref, go_ref, send_ref, at):
    cols = pl.ds(at, CB)
    nd = CB // 32
    row8 = lax.broadcasted_iota(jnp.int32, (8, CB), 0)
    feats, tails = [], []
    for b in range(3):
        feat, tail = featurize(
            br_ref[b, :, cols].astype(F32), [taps_ref[b, j : j + 1, cols] for j in range(3)]
        )
        feats.append(feat)
        tails.append(tail)
    query, key, value = feats
    go = go_ref[:, cols].astype(F32)
    products = (key * value).astype(BF16).T.reshape(nd, 32, CHUNK)
    gate_grad = (go * query).astype(BF16).T.reshape(nd, 32, CHUNK)
    heads = jnp.where(
        row8 < 2,
        query[:8],
        jnp.where(
            row8 < 4,
            pltpu.roll(key[:8], 2, 0),
            jnp.where(row8 < 6, pltpu.roll(value[:8], 4, 0), pltpu.roll(go[:8], 6, 0)),
        ),
    )
    ends = jnp.where(
        row8 < 2,
        tails[0],
        jnp.where(row8 < 4, pltpu.roll(tails[1], 2, 0), pltpu.roll(tails[2], 4, 0)),
    )
    quarter = lax.broadcasted_iota(jnp.int32, (8, CB), 1) // 8 % 4
    padded = []
    for q in range(4):
        padded += [jnp.where(quarter == q, heads, 0.0), jnp.where(quarter == q, ends, 0.0)]
    padded.append(jnp.zeros((CHUNK - 64, CB), F32))
    terms = jnp.concatenate(padded, axis=0).T.reshape(nd, 4, 8, CHUNK)
    terms = (terms[:, 0] + terms[:, 1] + terms[:, 2] + terms[:, 3]).astype(BF16)
    for n in range(nd):
        place = PLACE_IN[at // 32 + n]
        send_ref[place, 0:32, :] = products[n]
        send_ref[place, 32:64, :] = gate_grad[n]
        send_ref[place, 64:72, :] = terms[n]


def head_kernel(
    taps_hbm, br_hbm, go_hbm, send_hbm, taps_ref, br_ref, go_ref, send_ref, taps_sem, in_sem, out_sem
):
    channels = go_ref.shape[1]
    nd = CB // 32
    taps_copy = pltpu.make_async_copy(taps_slice(taps_hbm, channels), taps_ref, taps_sem)
    taps_copy.start()
    loads, stores = [], []
    for i in range(channels // CB):
        cols = pl.ds(i * CB, CB)
        loads.append(
            [
                pltpu.make_async_copy(
                    br_hbm.at[:, :, cols], br_ref.at[:, :, cols], in_sem.at[0, i]
                ),
                pltpu.make_async_copy(go_hbm.at[:, cols], go_ref.at[:, cols], in_sem.at[1, i]),
            ]
        )
        for copy in loads[-1]:
            copy.start()
    taps_copy.wait()
    for i in range(channels // CB):
        for copy in loads[i]:
            copy.wait()
        head_block(taps_ref, br_ref, go_ref, send_ref, i * CB)
        places = PLACE_IN[i * nd : (i + 1) * nd]
        out = pl.ds(min(places), nd)
        assert max(places) - min(places) == nd - 1
        stores.append(pltpu.make_async_copy(send_ref.at[out], send_hbm.at[out], out_sem.at[i]))
        stores[-1].start()
    for copy in stores:
        copy.wait()


def forward(signals, lhs1_ref, twist_ref, fwd_ref, apply):
    c, s = twist_ref[0], twist_ref[1]
    first = dot(lhs1_ref[...], jnp.concatenate(signals, axis=1))
    turned = []
    for ch in range(GROUP):
        at = 2 * HALF * ch
        for i in range(len(signals)):
            lanes = slice(CHUNK * i, CHUNK * (i + 1))
            re, im = first[at : at + HALF, lanes], first[at + HALF : at + 2 * HALF, lanes]
            pair = [(re * c - im * s).astype(BF16), (re * s + im * c).astype(BF16)]
            turned.append(jnp.concatenate(pair, axis=1))
    step = SPAN * len(signals)
    for at in range(0, len(turned), step):
        spectra = dot(jnp.concatenate(turned[at : at + step], axis=0), fwd_ref[...])
        for n in range(SPAN):
            parts = [
                spectra[HALF * (n * len(signals) + i) :][:HALF] for i in range(len(signals))
            ]
            apply(at // len(signals) + n, parts)


def backward(spectra, lhs2_ref, twist_ref, inv_ref):
    c, s = twist_ref[0], twist_ref[1]
    count = len(spectra[0])
    turned = []
    for at in range(0, GROUP, SPAN):
        flat = [x for channel in spectra[at : at + SPAN] for x in channel]
        value = dot(jnp.concatenate(flat, axis=0), inv_ref[...])
        for n in range(SPAN):
            res, ims = [], []
            for i in range(count):
                part = value[HALF * (n * count + i) :][:HALF]
                re, im = part[:, :CHUNK], part[:, CHUNK:]
                res.append((re * c + im * s).astype(BF16))
                ims.append((im * c - re * s).astype(BF16))
            turned.append(jnp.concatenate(res, axis=1))
            turned.append(jnp.concatenate(ims, axis=1))
    both = dot(lhs2_ref[...], jnp.concatenate(turned, axis=0))
    return [both[:, CHUNK * i : CHUNK * (i + 1)] for i in range(count)]


def filter_kernel(filter_ref, lhs1_ref, fwd_ref, twist_ref, out_ref):
    scale = (BLOCKS * CHUNK) ** -0.5
    for pair in range(2):
        signals = []
        for g in (2 * pair, 2 * pair + 1):
            rows = filter_ref[GROUP * g : GROUP * (g + 1), :] * scale
            stacked = [rows[:, CHUNK * m : CHUNK * (m + 1)] for m in ORDER_IN]
            signals.append(jnp.concatenate(stacked, axis=0).astype(BF16))

        def store(ch, parts):
            rows = slice(HALF * ch, HALF * (ch + 1))
            for i in range(2):
                out_ref[2 * pair + i, rows] = parts[i].astype(BF16)

        forward(signals, lhs1_ref, twist_ref, fwd_ref, store)


def middle_kernel(
    recv_ref,
    spec_ref,
    lhs1_ref,
    lhs2_ref,
    fwd_ref,
    inv_ref,
    twist_ref,
    send_hbm,
    corr_ref,
    send_ref,
    sems,
):
    shape = (BLOCKS, GROUP, CHUNK)
    flat = (BLOCKS * GROUP, CHUNK)
    lane = lax.broadcasted_iota(jnp.int32, (GROUP, CHUNK), 1)
    turn = lambda x, by: pltpu.roll(x, by % CHUNK, 2)
    halo = take(recv_ref[:, 64:72, :].astype(F32), PLACE_IN)
    before = jnp.concatenate([jnp.zeros((1, 8, CHUNK), F32), halo[:-1]], axis=0)
    feat = halo + turn(before, -8)
    prod = take(turn(feat, -2) * turn(feat, -4), ORDER_IN)
    gate = take(feat * turn(halo, -6), ORDER_IN)
    copies, outs, mixes = [], [], []
    join = lambda re, im: jnp.concatenate([re.astype(BF16), im.astype(BF16)], axis=1)
    for j in range(2):
        both = [recv_ref[:, at + 16 * j : at + 16 * (j + 1), :].astype(F32) for at in (0, 32)]
        for h in range(2):
            g = 2 * j + h
            rows = slice(GROUP * h, GROUP * (h + 1))
            signals = []
            for x, fix in zip(both, (prod, gate)):
                fixed = jnp.where(lane < 2, turn(fix, -SLOT * g), x[:, rows])
                signals.append(fixed.reshape(flat).astype(BF16))
            mixed = []

            def mix(ch, parts):
                rows = slice(HALF * ch, HALF * (ch + 1))
                (pr, pi), (gr, gi) = [(x[:, :CHUNK], x[:, CHUNK:]) for x in parts]
                hr = spec_ref[g, rows, :CHUNK].astype(F32)
                hi = spec_ref[g, rows, CHUNK:].astype(F32)
                corr_ref[g, rows] = join(pr * gr + pi * gi, pr * gi - pi * gr)
                mixed.append(
                    [
                        join(hr * pr - hi * pi, hr * pi + hi * pr),
                        join(hr * gr + hi * gi, hr * gi - hi * gr),
                    ]
                )

            forward(signals, lhs1_ref, twist_ref, fwd_ref, mix)
            mixes.append(mixed)
    for j in range(2):
        convs, dzetas = [], []
        for h in range(2):
            conv, dzeta = backward(mixes[2 * j + h], lhs2_ref, twist_ref, inv_ref)
            convs.append(conv.reshape(shape))
            dzetas.append(dzeta.reshape(shape))
        outs.append((convs, dzetas))
        for i in range(2):
            rows = slice(32 * i + 16 * j, 32 * i + 16 * (j + 1))
            send_ref[:, rows, :] = jnp.concatenate(outs[j][i], axis=1).astype(BF16)
            rows = pl.ds(32 * i + 16 * j, 16)
            copies.append(
                pltpu.make_async_copy(send_ref.at[:, rows], send_hbm.at[:, rows], sems.at[i, j])
            )
            copies[-1].start()
    merged = []
    for i in range(2):
        merged.append(outs[0][i][0])
        for g in range(1, 4):
            value = turn(outs[g // 2][i][g % 2], SLOT * g)
            merged[i] = jnp.where(lane < SLOT * g, merged[i], value)
    conv, dzeta = [take(x, PLACE_OUT) for x in merged]
    place = lane % SLOT
    heads = jnp.where(
        place < 2,
        conv * turn(halo, -6),
        jnp.where(place < 4, turn(dzeta, 2) * turn(feat, -2), turn(dzeta, 4) * turn(feat, 2)),
    )
    after = jnp.concatenate([heads[1:], jnp.zeros((1, 8, CHUNK), F32)], axis=0)
    terms = take(jnp.where(place < 8, feat, turn(after, 8)), ORDER_OUT)
    send_ref[:, 64:72, :] = terms.astype(BF16)
    rows = pl.ds(64, 8)
    copies.append(pltpu.make_async_copy(send_ref.at[:, rows], send_hbm.at[:, rows], sems.at[2, 0]))
    copies[-1].start()
    for copy in copies:
        copy.wait()


def grad_filter_kernel(
    taps_hbm,
    br_hbm,
    go_hbm,
    corr_ref,
    lhs2_ref,
    inv_ref,
    twist_ref,
    out_ref,
    taps_ref,
    rows_ref,
    br_ref,
    sems,
):
    channels = go_hbm.shape[1]
    copies = [
        pltpu.make_async_copy(taps_slice(taps_hbm, channels), taps_ref, sems.at[0]),
        pltpu.make_async_copy(br_hbm.at[1:3], br_ref, sems.at[1]),
        pltpu.make_async_copy(go_hbm, rows_ref.at[2], sems.at[2]),
    ]
    for copy in copies:
        copy.start()
    for copy in copies:
        copy.wait()
    for i in range(channels // CB):
        cols = pl.ds(i * CB, CB)
        for b in range(2):
            taps = [taps_ref[b + 1, j : j + 1, cols] for j in range(3)]
            rows_ref[b, :, cols] = featurize(br_ref[b, :, cols].astype(F32), taps)[0].astype(BF16)
    scale = (BLOCKS * CHUNK) ** -0.5
    for pair in range(2):
        spectra = [
            [corr_ref[2 * pair + i, HALF * ch : HALF * (ch + 1)] for i in range(2)]
            for ch in range(GROUP)
        ]
        values = backward(spectra, lhs2_ref, twist_ref, inv_ref)
        for i in range(2):
            at = GROUP * (2 * pair + i)
            for n, m in enumerate(ORDER_OUT):
                out_ref[at : at + GROUP, CHUNK * m : CHUNK * (m + 1)] = (
                    values[i][GROUP * n : GROUP * (n + 1)] * scale
                )


def tail_block(taps_ref, rows_ref, recv_ref, out_ref, at):
    cols = pl.ds(at, CB)
    row8 = lax.broadcasted_iota(jnp.int32, (8, CB), 0)
    places = PLACE_OUT[at // 32 : (at + CB) // 32]
    received = lambda rows: jnp.stack([recv_ref[p, rows, :] for p in places])
    conv = received(slice(0, 32)).reshape(CB, CHUNK).T.astype(F32)
    dzeta = received(slice(32, 64)).reshape(CB, CHUNK).T.astype(F32)
    halo = received(slice(64, 72)).astype(F32)
    turned = [halo] + [pltpu.roll(halo, CHUNK - SLOT * q, 2) for q in range(1, 4)]
    halo = jnp.concatenate(turned, axis=1).reshape(CB, CHUNK).T
    heads, nexts = halo[:8], halo[8:16]

    def with_head(b, at):
        value = rows_ref[b, :, cols].astype(F32)
        first = jnp.where(row8 < 2, pltpu.roll(heads, 8 - at, 0), value[:8])
        return jnp.concatenate([first, value[8:]], axis=0)

    key = with_head(0, 2)
    value = with_head(1, 4)
    grads = (rows_ref[2, :, cols].astype(F32) * conv, dzeta * value, dzeta * key)
    for b in range(3):
        d = grads[b]
        s0, s1, s2 = (taps_ref[b, j : j + 1, cols] for j in range(3))
        d1 = pltpu.roll(d, CHUNK - 1, 0)
        d2 = pltpu.roll(d, CHUNK - 2, 0)
        e1 = jnp.where(row8 < 7, d1[-8:], pltpu.roll(nexts, (7 - 2 * b) % 8, 0))
        e2 = jnp.where(row8 < 6, d2[-8:], pltpu.roll(nexts, (6 - 2 * b) % 8, 0))
        d1 = jnp.concatenate([d1[:-8], e1], axis=0)
        d2 = jnp.concatenate([d2[:-8], e2], axis=0)
        out_ref[b, :, cols] = (s0 * d + s1 * d1 + s2 * d2).astype(BF16)


def tail_kernel(taps_ref, rows_ref, recv_ref, out_hbm, out_ref, sem):
    stores = []
    for i in range(out_ref.shape[2] // CB):
        tail_block(taps_ref, rows_ref, recv_ref, out_ref, i * CB)
        cols = pl.ds(i * CB, CB)
        stores.append(
            pltpu.make_async_copy(out_ref.at[:, :, cols], out_hbm.at[:, :, cols], sem.at[i])
        )
        stores[-1].start()
    for copy in stores:
        copy.wait()


def params(mib):
    return pltpu.CompilerParams(vmem_limit_bytes=mib << 20)


def exchange(x, order):
    return lax.all_to_all(
        x, "ctx", split_axis=0, concat_axis=0, axis_index_groups=[order], tiled=True
    )


def per_device(branches, short_taps, long_filter, grad_out):
    lhs1, lhs2, fwd, inv, twist = (jnp.asarray(t) for t in tables())
    tokens, channels = grad_out.shape
    steps = channels // CB
    half = GROUP * HALF
    hbm = pl.BlockSpec(memory_space=pltpu.HBM)
    vmem = pl.BlockSpec(memory_space=pltpu.VMEM)
    dma = pltpu.SemaphoreType.DMA
    wire = (BLOCKS, ROWS, CHUNK)
    spectral = (32 // GROUP, half, 2 * CHUNK)
    held = lambda x: pltpu.with_memory_space_constraint(x, pltpu.HBM)
    branches, short_taps, grad_out = map(held, (branches, short_taps, grad_out))
    send = pl.pallas_call(
        head_kernel,
        in_specs=[hbm, hbm, hbm],
        out_specs=hbm,
        out_shape=pltpu.HBM(wire, BF16),
        scratch_shapes=[
            pltpu.VMEM((3, 3, channels), F32),
            pltpu.VMEM((3, tokens, channels), BF16),
            pltpu.VMEM((tokens, channels), BF16),
            pltpu.VMEM(wire, BF16),
            dma,
            dma((2, steps)),
            dma((steps,)),
        ],
        compiler_params=params(24),
        name="head",
    )(short_taps, branches, grad_out)
    spectrum = pl.pallas_call(
        filter_kernel,
        in_specs=[vmem] * 4,
        out_specs=vmem,
        out_shape=pltpu.VMEM(spectral, BF16),
        compiler_params=params(32),
        name="filter_spectrum",
    )(long_filter, lhs1, fwd, twist)
    recv = exchange(send, ORDER_IN)
    back, corr = pl.pallas_call(
        middle_kernel,
        in_specs=[vmem] * 7,
        out_specs=[hbm, vmem],
        out_shape=[pltpu.HBM(wire, BF16), pltpu.VMEM(spectral, BF16)],
        scratch_shapes=[pltpu.VMEM(wire, BF16), dma((3, 2))],
        compiler_params=params(32),
        name="middle",
    )(recv, spectrum, lhs1, lhs2, fwd, inv, twist)
    grad_filter, taps, rows = pl.pallas_call(
        grad_filter_kernel,
        in_specs=[hbm, hbm, hbm, vmem, vmem, vmem, vmem],
        out_specs=[vmem, vmem, vmem],
        out_shape=[
            jax.ShapeDtypeStruct(long_filter.shape, F32),
            pltpu.VMEM((3, 3, channels), F32),
            pltpu.VMEM((3, tokens, channels), BF16),
        ],
        scratch_shapes=[
            pltpu.VMEM((2, tokens, channels), BF16),
            dma((3,)),
        ],
        compiler_params=params(32),
        name="grad_filter",
    )(short_taps, branches, grad_out, corr, lhs2, inv, twist)
    returned = exchange(back, ORDER_OUT)
    grads = pl.pallas_call(
        tail_kernel,
        in_specs=[vmem, vmem, vmem],
        out_specs=hbm,
        out_shape=pltpu.HBM(branches.shape, BF16),
        scratch_shapes=[pltpu.VMEM(branches.shape, BF16), dma((steps,))],
        compiler_params=params(24),
        name="tail",
    )(taps, rows, returned)
    return grads, grad_filter


def solution(mesh):
    in_specs = (P(None, "ctx", "tp"), P(), P(("tp", "ctx"), None), P("ctx", "tp"))
    out_specs = (P(None, "ctx", "tp"), P(("tp", "ctx"), None))
    return jax.shard_map(
        per_device, mesh=mesh, in_specs=in_specs, out_specs=out_specs, check_vma=False
    )
```

time: 54.1 us -> 46.3 us (0.86)
  waiting for transfers between devices: 24 us -> 10.3 us
  starting transfers between devices: 14.9 us -> 23.9 us
  Pallas kernels: 14 us -> 10.5 us
    all_to_all x2, waiting for transfers between devices: 24 us -> 10.3 us  [exchange(): lax.all_to_all(x, 'ctx', split_axis=0, concat_axis=0, axis_index_groups=[...]
    all_to_all x2, starting transfers between devices: 14.9 us -> 23.9 us  [exchange(): lax.all_to_all(x, 'ctx', split_axis=0, concat_axis=0, axis_index_groups=[...]
    pallas_call x2, Pallas kernels: 7.79 us -> 5.47 us  [the longest x1 2.86 us: per_device(): pl.pallas_call(grad_filter_kernel, in_specs=[hbm, hbm, hbm, vmem, vmem, v...]
    pallas_call x1, Pallas kernels: 1.48 us -> 0.55 us  [per_device(): pl.pallas_call(filter_kernel, in_specs=[vmem] * 4, out_specs=vmem, out_sh...]
  transfers between devices with their start and end apart: 2 -> 2, of which waited for: 2 -> 2; matrix products, arithmetic and copies ran while one was open for 0% -> 0% of each run, Pallas kernels for 9% -> 7%
where the time goes in v2:
time: 46.3 us; the launch traced here: 45.5 us
  starting transfers between devices  23.9 us (52%)
  Pallas kernels  10.5 us (23%)
  waiting for transfers between devices  10.3 us (22%)
  between operations  0.76 us (2%)
    all_to_all x2, starting transfers between devices, exchange(): lax.all_to_all(x, 'ctx', split_axis=0, concat_axis=0, axis_index_groups=[...  23.9 us
    all_to_all x2, waiting for transfers between devices, exchange(): lax.all_to_all(x, 'ctx', split_axis=0, concat_axis=0, axis_index_groups=[...  10.3 us
    pallas_call x1, Pallas kernels, per_device(): pl.pallas_call(head_kernel, in_specs=[hbm, hbm, hbm], out_specs=hbm, out_...  2.97 us
    pallas_call x1, Pallas kernels, per_device(): pl.pallas_call(grad_filter_kernel, in_specs=[hbm, hbm, hbm, vmem, vmem, v...  2.86 us
    pallas_call x1, Pallas kernels, per_device(): pl.pallas_call(middle_kernel, in_specs=[vmem] * 7, out_specs=[hbm, vmem],...  2.61 us
    pallas_call x1, Pallas kernels, per_device(): pl.pallas_call(tail_kernel, in_specs=[vmem, vmem, vmem], out_specs=hbm, o...  1.51 us
  transfers between devices with their start and end apart: 2, of which 2 were waited for; matrix products, arithmetic and copies ran while one was open for 0% of the time, Pallas kernels for 7%

profile of v2, /device:TPU:0, one launch (start us, length us, event | category | flops | bytes accessed | tf_op | source)
XLA Modules:
  0.0 45.5 jit_solution(1458594685157493632)
XLA Ops:
  0.6 3.0 %head.1 = bf16[32,72,128]{2,1,0:T(8,128)(2,1)} custom-call(f32[3,3,4096]{2,1,0:T(4,128)} %taps_hbm.3, bf16[3,128,1024]{2,1,0:T(8,128)(2,1)} %br_hbm.3, bf16[128,1024]{1,0:T(8,128)(2,1)} %go_hbm.3), custom_call_target="tpu_custom_call" | custom-call | tf_op jit(solution)/shard_map/head/pallas_call | solution.py:408
  3.6 0.0 copy-start.1
  3.6 0.0 copy-start.2
  3.6 0.0 copy-start.4
  3.6 0.0 copy-start.5
  3.7 13.0 %all-to-all-start = ((bf16[32,72,128]{2,1,0:T(8,128)(2,1)}), bf16[32,72,128]{2,1,0:T(8,128)(2,1)S(1)}, u32[]{:S(2)}, u32[]{:S(2)}) async-start(bf16[32,72,128]{2,1,0:T(8,128)(2,1)} %head.1), calls=%async_computation | async-start | bytes 1179648 | tf_op jit(solution)/shard_map/all_to_all | solution.py:391
  16.7 0.0 copy-done.1
  16.7 0.0 copy-done.2
  16.7 0.0 copy-done.4
  16.7 0.0 copy-done.5
  16.7 0.0 copy-start
  16.7 0.0 copy-start.3
  16.7 0.6 %filter_spectrum.1.spec_ref = bf16[4,256,256]{2,1,0:T(8,128)(2,1)S(1)} custom-call(f32[32,4096]{1,0:T(8,128)S(1)} %copy-done.2, bf16[512,256]{1,0:T(8,128)(2,1)S(1)} %copy-done.1, bf16[256,256]{1,0:T(8,128)(2,1)S(1)} %copy-done.4, f32[2,32,128]{2,1,0:T(8,128)S(1)} %copy-done.5), custom_call_target="tpu_custom_call" | custom-call | tf_op jit(solution)/shard_map/filter_spectrum/pallas_call | solution.py:425
  17.3 6.6 %all-to-all-done.recv_ref = bf16[32,72,128]{2,1,0:T(8,128)(2,1)S(1)} async-done(((bf16[32,72,128]{2,1,0:T(8,128)(2,1)}), bf16[32,72,128]{2,1,0:T(8,128)(2,1)S(1)}, u32[]{:S(2)}, u32[]{:S(2)}) %all-to-all-start) | async-done | bytes 589856 | tf_op jit(solution)/shard_map/all_to_all | solution.py:391
  23.9 0.0 copy-done
  23.9 0.0 copy-done.3
  23.9 2.6 %middle.1 = (bf16[32,72,128]{2,1,0:T(8,128)(2,1)}, bf16[4,256,256]{2,1,0:T(8,128)(2,1)S(1)}) custom-call(bf16[32,72,128]{2,1,0:T(8,128)(2,1)S(1)} %all-to-all-done.recv_ref, bf16[4,256,256]{2,1,0:T(8,128)(2,1)S(1)} %filter_spectrum.1.spec_ref, bf16[512,256]{1,0:T(8,128)(2,1)S(1)} %copy-done.1, bf16[256,512]{1,0:T(8,128)(2,1)S(1)} %copy-done, ...), custom_call_target="tpu_custom_call" | custom-call | tf_op jit(solution)/shard_map/middle/pallas_call | solution.py:434
  26.5 10.9 %all-to-all-start.1 = ((bf16[32,72,128]{2,1,0:T(8,128)(2,1)}), bf16[32,72,128]{2,1,0:T(8,128)(2,1)S(1)}, u32[]{:S(2)}, u32[]{:S(2)}) async-start(bf16[32,72,128]{2,1,0:T(8,128)(2,1)} %get-tuple-element.10), calls=%async_computation.1 | async-start | bytes 1179648 | tf_op jit(solution)/shard_map/all_to_all | solution.py:391
  37.4 2.9 %grad_filter.1 = (f32[32,4096]{1,0:T(8,128)}, f32[3,3,1024]{2,1,0:T(4,128)S(1)}, bf16[3,128,1024]{2,1,0:T(8,128)(2,1)S(1)}) custom-call(f32[3,3,4096]{2,1,0:T(4,128)} %taps_hbm.3, bf16[3,128,1024]{2,1,0:T(8,128)(2,1)} %br_hbm.3, bf16[128,1024]{1,0:T(8,128)(2,1)} %go_hbm.3, bf16[4,256,256]{2,1,0:T(8,128)(2,1)S(1)} %get-tuple-element.7.corr_ref, ...), custom_call_target="tpu_custom_call" | custom-call | tf_op jit(solution)/shard_map/grad_filter/pallas_call | solution.py:443
  40.3 3.7 %all-to-all-done.1.recv_ref = bf16[32,72,128]{2,1,0:T(8,128)(2,1)S(1)} async-done(((bf16[32,72,128]{2,1,0:T(8,128)(2,1)}), bf16[32,72,128]{2,1,0:T(8,128)(2,1)S(1)}, u32[]{:S(2)}, u32[]{:S(2)}) %all-to-all-start.1) | async-done | bytes 589856 | tf_op jit(solution)/shard_map/all_to_all | solution.py:391
  43.9 1.5 %tail.1 = bf16[3,128,1024]{2,1,0:T(8,128)(2,1)} custom-call(f32[3,3,1024]{2,1,0:T(4,128)S(1)} %get-tuple-element.8.taps_ref, bf16[3,128,1024]{2,1,0:T(8,128)(2,1)S(1)} %get-tuple-element.9.rows_ref, bf16[32,72,128]{2,1,0:T(8,128)(2,1)S(1)} %all-to-all-done.1.recv_ref), custom_call_target="tpu_custom_call" | custom-call | tf_op jit(solution)/shard_map/tail/pallas_call | solution.py:460
Async XLA Ops:
  3.6 13.0 %copy-start.1 = (bf16[512,256]{1,0:T(8,128)(2,1)S(1)}, bf16[512,256]{1,0:T(8,128)(2,1)}, u32[]{:S(2)}) copy-start(bf16[512,256]{1,0:T(8,128)(2,1)} %constant.10.clone.lhs1_ref) | copy-start | bytes 786436
  3.6 13.0 %copy-start.2 = (f32[32,4096]{1,0:T(8,128)S(1)}, f32[32,4096]{1,0:T(8,128)}, u32[]{:S(2)}) copy-start(f32[32,4096]{1,0:T(8,128)} %filter_ref.1) | copy-start | bytes 1572868
  3.6 13.0 %copy-start.4 = (bf16[256,256]{1,0:T(8,128)(2,1)S(1)}, bf16[256,256]{1,0:T(8,128)(2,1)}, u32[]{:S(2)}) copy-start(bf16[256,256]{1,0:T(8,128)(2,1)} %constant.12.clone.fwd_ref) | copy-start | bytes 393220
  3.6 13.0 %copy-start.5 = (f32[2,32,128]{2,1,0:T(8,128)S(1)}, f32[2,32,128]{2,1,0:T(8,128)}, u32[]{:S(2)}) copy-start(f32[2,32,128]{2,1,0:T(8,128)} %constant.14.clone.twist_ref) | copy-start | bytes 98308
  3.7 20.2 %all-to-all-start = ((bf16[32,72,128]{2,1,0:T(8,128)(2,1)}), bf16[32,72,128]{2,1,0:T(8,128)(2,1)S(1)}, u32[]{:S(2)}, u32[]{:S(2)}) async-start(bf16[32,72,128]{2,1,0:T(8,128)(2,1)} %head.1), calls=%async_computation | async-start | bytes 1179648 | tf_op jit(solution)/shard_map/all_to_all | solution.py:391
  16.7 7.2 %copy-start = (bf16[256,512]{1,0:T(8,128)(2,1)S(1)}, bf16[256,512]{1,0:T(8,128)(2,1)}, u32[]{:S(2)}) copy-start(bf16[256,512]{1,0:T(8,128)(2,1)} %constant.11.clone.lhs2_ref) | copy-start | bytes 786436
  16.7 7.2 %copy-start.3 = (bf16[256,256]{1,0:T(8,128)(2,1)S(1)}, bf16[256,256]{1,0:T(8,128)(2,1)}, u32[]{:S(2)}) copy-start(bf16[256,256]{1,0:T(8,128)(2,1)} %constant.13.clone.inv_ref) | copy-start | bytes 393220
  26.5 17.4 %all-to-all-start.1 = ((bf16[32,72,128]{2,1,0:T(8,128)(2,1)}), bf16[32,72,128]{2,1,0:T(8,128)(2,1)S(1)}, u32[]{:S(2)}, u32[]{:S(2)}) async-start(bf16[32,72,128]{2,1,0:T(8,128)(2,1)} %get-tuple-element.10), calls=%async_computation.1 | async-start | bytes 1179648 | tf_op jit(solution)/shard_map/all_to_all | solution.py:391

commit v3 on v2

--- a/solution.py
+++ b/solution.py
@@ -14,15 +14,20 @@
 CHUNK = 128
 BLOCKS = 32
 GROUP = 8
-SPAN = 8
 SLOT = 16
 HALF = BLOCKS
 PERIOD = 2 * BLOCKS * CHUNK
 ROWS = 72
 CB = 256
 
-ORDER_IN = [i ^ 21 for i in range(BLOCKS)]
-ORDER_OUT = [i ^ 21 for i in range(BLOCKS)]
+
+def ctx_order():
+    lexical = [8 * z + 2 * y + x for y in range(4) for x in range(2) for z in range(4)]
+    return [lexical[13 * j % BLOCKS] ^ 21 for j in range(BLOCKS)]
+
+
+ORDER_IN = ctx_order()
+ORDER_OUT = ctx_order()
 PLACE_IN = [ORDER_IN.index(i) for i in range(BLOCKS)]
 PLACE_OUT = [ORDER_OUT.index(i) for i in range(BLOCKS)]
 
@@ -52,6 +57,16 @@
     return jnp.concatenate([x[i : i + 1] for i in order], axis=0)
 
 
+def runs(places):
+    found = []
+    for p in sorted(places):
+        if found and sum(found[-1]) == p:
+            found[-1] = (found[-1][0], found[-1][1] + 1)
+        else:
+            found.append((p, 1))
+    return found
+
+
 def dot(a, b):
     return jnp.dot(a, b, preferred_element_type=F32)
 
@@ -61,29 +76,30 @@
 
 
 def featurize(x, taps):
-    row = lax.broadcasted_iota(jnp.int32, x.shape, 0)
     s0, s1, s2 = taps
     x1 = pltpu.roll(x, 1, 0)
     x2 = pltpu.roll(x, 2, 0)
-    feat = s0 * x + s1 * jnp.where(row < 1, 0.0, x1) + s2 * jnp.where(row < 2, 0.0, x2)
-    row = row[:8]
-    tail = jnp.where(row < 1, s1 * x1[:8], 0.0) + jnp.where(row < 2, s2 * x2[:8], 0.0)
-    return feat, tail
-
-
-def head_block(taps_ref, br_ref, go_ref, send_ref, at):
+    feat = s0 * x[8:] + s1 * x1[8:] + s2 * x2[8:]
+    row = lax.broadcasted_iota(jnp.int32, (8, x.shape[1]), 0)
+    one, two = s1 * x1[:8], s2 * x2[:8]
+    first = s0 * x[:8] + jnp.where(row < 1, 0.0, one) + jnp.where(row < 2, 0.0, two)
+    tail = jnp.where(row < 1, one, 0.0) + jnp.where(row < 2, two, 0.0)
+    return jnp.concatenate([first, feat], axis=0), tail
+
+
+def head_block(taps_ref, rows_ref, send_ref, at):
     cols = pl.ds(at, CB)
     nd = CB // 32
     row8 = lax.broadcasted_iota(jnp.int32, (8, CB), 0)
     feats, tails = [], []
     for b in range(3):
         feat, tail = featurize(
-            br_ref[b, :, cols].astype(F32), [taps_ref[b, j : j + 1, cols] for j in range(3)]
+            rows_ref[b, :, cols].astype(F32), [taps_ref[b, j : j + 1, cols] for j in range(3)]
         )
         feats.append(feat)
         tails.append(tail)
     query, key, value = feats
-    go = go_ref[:, cols].astype(F32)
+    go = rows_ref[3, :, cols].astype(F32)
     products = (key * value).astype(BF16).T.reshape(nd, 32, CHUNK)
     gate_grad = (go * query).astype(BF16).T.reshape(nd, 32, CHUNK)
     heads = jnp.where(
@@ -115,40 +131,29 @@
 
 
 def head_kernel(
-    taps_hbm, br_hbm, go_hbm, send_hbm, taps_ref, br_ref, go_ref, send_ref, taps_sem, in_sem, out_sem
+    taps_hbm, br_hbm, go_hbm, send_hbm, taps_ref, rows_ref, send_ref, taps_sem, in_sem, out_sem
 ):
-    channels = go_ref.shape[1]
+    channels = rows_ref.shape[2]
     nd = CB // 32
     taps_copy = pltpu.make_async_copy(taps_slice(taps_hbm, channels), taps_ref, taps_sem)
     taps_copy.start()
-    loads, stores = [], []
-    for i in range(channels // CB):
-        cols = pl.ds(i * CB, CB)
-        loads.append(
-            [
-                pltpu.make_async_copy(
-                    br_hbm.at[:, :, cols], br_ref.at[:, :, cols], in_sem.at[0, i]
-                ),
-                pltpu.make_async_copy(go_hbm.at[:, cols], go_ref.at[:, cols], in_sem.at[1, i]),
-            ]
-        )
-        for copy in loads[-1]:
-            copy.start()
+    blocks = [pl.ds(i * CB, CB) for i in range(channels // CB)]
+    for i, cols in enumerate(blocks):
+        dst = rows_ref.at[0:3, :, cols]
+        pltpu.make_async_copy(br_hbm.at[:, :, cols], dst, in_sem.at[i]).start()
+        pltpu.make_async_copy(go_hbm.at[:, cols], rows_ref.at[3, :, cols], in_sem.at[i]).start()
     taps_copy.wait()
-    for i in range(channels // CB):
-        for copy in loads[i]:
-            copy.wait()
-        head_block(taps_ref, br_ref, go_ref, send_ref, i * CB)
-        places = PLACE_IN[i * nd : (i + 1) * nd]
-        out = pl.ds(min(places), nd)
-        assert max(places) - min(places) == nd - 1
-        stores.append(pltpu.make_async_copy(send_ref.at[out], send_hbm.at[out], out_sem.at[i]))
-        stores[-1].start()
-    for copy in stores:
-        copy.wait()
-
-
-def forward(signals, lhs1_ref, twist_ref, fwd_ref, apply):
+    for i, cols in enumerate(blocks):
+        both = rows_ref.at[:, :, cols]
+        pltpu.make_async_copy(both, both, in_sem.at[i]).wait()
+        head_block(taps_ref, rows_ref, send_ref, i * CB)
+        for first, length in runs(PLACE_IN[i * nd : (i + 1) * nd]):
+            out = pl.ds(first, length)
+            pltpu.make_async_copy(send_ref.at[out], send_hbm.at[out], out_sem).start()
+    pltpu.make_async_copy(send_ref, send_hbm, out_sem).wait()
+
+
+def spread(signals, lhs1_ref, twist_ref):
     c, s = twist_ref[0], twist_ref[1]
     first = dot(lhs1_ref[...], jnp.concatenate(signals, axis=1))
     turned = []
@@ -159,33 +164,35 @@
             re, im = first[at : at + HALF, lanes], first[at + HALF : at + 2 * HALF, lanes]
             pair = [(re * c - im * s).astype(BF16), (re * s + im * c).astype(BF16)]
             turned.append(jnp.concatenate(pair, axis=1))
-    step = SPAN * len(signals)
-    for at in range(0, len(turned), step):
-        spectra = dot(jnp.concatenate(turned[at : at + step], axis=0), fwd_ref[...])
-        for n in range(SPAN):
-            parts = [
-                spectra[HALF * (n * len(signals) + i) :][:HALF] for i in range(len(signals))
-            ]
-            apply(at // len(signals) + n, parts)
+    return jnp.concatenate(turned, axis=0)
+
+
+def forward(signals, lhs1_ref, twist_ref, fwd_ref, apply):
+    count = len(signals)
+    spectra = dot(spread(signals, lhs1_ref, twist_ref), fwd_ref[...])
+    for n in range(GROUP):
+        apply(n, [spectra[HALF * (n * count + i) :][:HALF] for i in range(count)])
+
+
+def gather(value, count, twist_ref):
+    c, s = twist_ref[0], twist_ref[1]
+    turned = []
+    for n in range(GROUP):
+        res, ims = [], []
+        for i in range(count):
+            part = value[HALF * (n * count + i) :][:HALF]
+            re, im = part[:, :CHUNK], part[:, CHUNK:]
+            res.append((re * c + im * s).astype(BF16))
+            ims.append((im * c - re * s).astype(BF16))
+        turned.append(jnp.concatenate(res, axis=1))
+        turned.append(jnp.concatenate(ims, axis=1))
+    return jnp.concatenate(turned, axis=0)
 
 
 def backward(spectra, lhs2_ref, twist_ref, inv_ref):
-    c, s = twist_ref[0], twist_ref[1]
     count = len(spectra[0])
-    turned = []
-    for at in range(0, GROUP, SPAN):
-        flat = [x for channel in spectra[at : at + SPAN] for x in channel]
-        value = dot(jnp.concatenate(flat, axis=0), inv_ref[...])
-        for n in range(SPAN):
-            res, ims = [], []
-            for i in range(count):
-                part = value[HALF * (n * count + i) :][:HALF]
-                re, im = part[:, :CHUNK], part[:, CHUNK:]
-                res.append((re * c + im * s).astype(BF16))
-                ims.append((im * c - re * s).astype(BF16))
-            turned.append(jnp.concatenate(res, axis=1))
-            turned.append(jnp.concatenate(ims, axis=1))
-    both = dot(lhs2_ref[...], jnp.concatenate(turned, axis=0))
+    value = dot(jnp.concatenate([x for ch in spectra for x in ch], axis=0), inv_ref[...])
+    both = dot(lhs2_ref[...], gather(value, count, twist_ref))
     return [both[:, CHUNK * i : CHUNK * (i + 1)] for i in range(count)]
 
 
@@ -217,7 +224,7 @@
     send_hbm,
     corr_ref,
     send_ref,
-    sems,
+    sem,
 ):
     shape = (BLOCKS, GROUP, CHUNK)
     flat = (BLOCKS * GROUP, CHUNK)
@@ -228,7 +235,7 @@
     feat = halo + turn(before, -8)
     prod = take(turn(feat, -2) * turn(feat, -4), ORDER_IN)
     gate = take(feat * turn(halo, -6), ORDER_IN)
-    copies, outs, mixes = [], [], []
+    outs, mixes, spreads = [], [], []
     join = lambda re, im: jnp.concatenate([re.astype(BF16), im.astype(BF16)], axis=1)
     for j in range(2):
         both = [recv_ref[:, at + 16 * j : at + 16 * (j + 1), :].astype(F32) for at in (0, 32)]
@@ -239,38 +246,37 @@
             for x, fix in zip(both, (prod, gate)):
                 fixed = jnp.where(lane < 2, turn(fix, -SLOT * g), x[:, rows])
                 signals.append(fixed.reshape(flat).astype(BF16))
-            mixed = []
-
-            def mix(ch, parts):
-                rows = slice(HALF * ch, HALF * (ch + 1))
-                (pr, pi), (gr, gi) = [(x[:, :CHUNK], x[:, CHUNK:]) for x in parts]
-                hr = spec_ref[g, rows, :CHUNK].astype(F32)
-                hi = spec_ref[g, rows, CHUNK:].astype(F32)
-                corr_ref[g, rows] = join(pr * gr + pi * gi, pr * gi - pi * gr)
-                mixed.append(
-                    [
-                        join(hr * pr - hi * pi, hr * pi + hi * pr),
-                        join(hr * gr + hi * gi, hr * gi - hi * gr),
-                    ]
-                )
-
-            forward(signals, lhs1_ref, twist_ref, fwd_ref, mix)
-            mixes.append(mixed)
+            spreads.append(spread(signals, lhs1_ref, twist_ref))
+    size = 2 * GROUP * HALF
+    everything = dot(jnp.concatenate(spreads, axis=0), fwd_ref[...])
+    for g in range(4):
+        spectra = everything[size * g : size * (g + 1)]
+        mixed = []
+        for ch in range(GROUP):
+            at = 2 * HALF * ch
+            parts = (spectra[at : at + HALF], spectra[at + HALF : at + 2 * HALF])
+            (pr, pi), (gr, gi) = [(x[:, :CHUNK], x[:, CHUNK:]) for x in parts]
+            rows = slice(HALF * ch, HALF * (ch + 1))
+            hr = spec_ref[g, rows, :CHUNK].astype(F32)
+            hi = spec_ref[g, rows, CHUNK:].astype(F32)
+            corr_ref[g, rows] = join(pr * gr + pi * gi, pr * gi - pi * gr)
+            mixed.append(join(hr * pr - hi * pi, hr * pi + hi * pr))
+            mixed.append(join(hr * gr + hi * gi, hr * gi - hi * gr))
+        mixes.append(jnp.concatenate(mixed, axis=0))
+    everything = dot(jnp.concatenate(mixes, axis=0), inv_ref[...])
+    gathers = [gather(everything[size * g : size * (g + 1)], 2, twist_ref) for g in range(4)]
     for j in range(2):
         convs, dzetas = [], []
         for h in range(2):
-            conv, dzeta = backward(mixes[2 * j + h], lhs2_ref, twist_ref, inv_ref)
-            convs.append(conv.reshape(shape))
-            dzetas.append(dzeta.reshape(shape))
+            value = dot(lhs2_ref[...], gathers[2 * j + h])
+            convs.append(value[:, :CHUNK].reshape(shape))
+            dzetas.append(value[:, CHUNK:].reshape(shape))
         outs.append((convs, dzetas))
         for i in range(2):
             rows = slice(32 * i + 16 * j, 32 * i + 16 * (j + 1))
             send_ref[:, rows, :] = jnp.concatenate(outs[j][i], axis=1).astype(BF16)
             rows = pl.ds(32 * i + 16 * j, 16)
-            copies.append(
-                pltpu.make_async_copy(send_ref.at[:, rows], send_hbm.at[:, rows], sems.at[i, j])
-            )
-            copies[-1].start()
+            pltpu.make_async_copy(send_ref.at[:, rows], send_hbm.at[:, rows], sem).start()
     merged = []
     for i in range(2):
         merged.append(outs[0][i][0])
@@ -288,10 +294,8 @@
     terms = take(jnp.where(place < 8, feat, turn(after, 8)), ORDER_OUT)
     send_ref[:, 64:72, :] = terms.astype(BF16)
     rows = pl.ds(64, 8)
-    copies.append(pltpu.make_async_copy(send_ref.at[:, rows], send_hbm.at[:, rows], sems.at[2, 0]))
-    copies[-1].start()
-    for copy in copies:
-        copy.wait()
+    pltpu.make_async_copy(send_ref.at[:, rows], send_hbm.at[:, rows], sem).start()
+    pltpu.make_async_copy(send_ref, send_hbm, sem).wait()
 
 
 def grad_filter_kernel(
@@ -371,16 +375,11 @@
 
 
 def tail_kernel(taps_ref, rows_ref, recv_ref, out_hbm, out_ref, sem):
-    stores = []
     for i in range(out_ref.shape[2] // CB):
         tail_block(taps_ref, rows_ref, recv_ref, out_ref, i * CB)
         cols = pl.ds(i * CB, CB)
-        stores.append(
-            pltpu.make_async_copy(out_ref.at[:, :, cols], out_hbm.at[:, :, cols], sem.at[i])
-        )
-        stores[-1].start()
-    for copy in stores:
-        copy.wait()
+        pltpu.make_async_copy(out_ref.at[:, :, cols], out_hbm.at[:, :, cols], sem).start()
+    pltpu.make_async_copy(out_ref, out_hbm, sem).wait()
 
 
 def params(mib):
@@ -412,12 +411,11 @@
         out_shape=pltpu.HBM(wire, BF16),
         scratch_shapes=[
             pltpu.VMEM((3, 3, channels), F32),
-            pltpu.VMEM((3, tokens, channels), BF16),
-            pltpu.VMEM((tokens, channels), BF16),
+            pltpu.VMEM((4, tokens, channels), BF16),
             pltpu.VMEM(wire, BF16),
             dma,
-            dma((2, steps)),
             dma((steps,)),
+            dma,
         ],
         compiler_params=params(24),
         name="head",
@@ -436,7 +434,7 @@
         in_specs=[vmem] * 7,
         out_specs=[hbm, vmem],
         out_shape=[pltpu.HBM(wire, BF16), pltpu.VMEM(spectral, BF16)],
-        scratch_shapes=[pltpu.VMEM(wire, BF16), dma((3, 2))],
+        scratch_shapes=[pltpu.VMEM(wire, BF16), dma],
         compiler_params=params(32),
         name="middle",
     )(recv, spectrum, lhs1, lhs2, fwd, inv, twist)
@@ -462,7 +460,7 @@
         in_specs=[vmem, vmem, vmem],
         out_specs=hbm,
         out_shape=pltpu.HBM(branches.shape, BF16),
-        scratch_shapes=[pltpu.VMEM(branches.shape, BF16), dma((steps,))],
+        scratch_shapes=[pltpu.VMEM(branches.shape, BF16), dma],
         compiler_params=params(24),
         name="tail",
     )(taps, rows, returned)

time: 46.3 us -> 44.8 us (0.968); the launches traced: 45.5 us -> 44.5 us
  waiting for transfers between devices: 10.3 us -> 9.16 us
    all_to_all x2, waiting for transfers between devices: 10.3 us -> 9.16 us  [exchange(): lax.all_to_all(x, 'ctx', split_axis=0, concat_axis=0, axis_index_groups=[...]
  transfers between devices with their start and end apart: 2 -> 2, of which waited for: 2 -> 2; matrix products, arithmetic and copies ran while one was open for 0% -> 0% of each run, Pallas kernels for 7% -> 8%
where the time goes in v3:
time: 44.8 us; the launch traced here: 44.5 us
  starting transfers between devices  24.2 us (54%)
  Pallas kernels  10.3 us (23%)
  waiting for transfers between devices  9.16 us (20%)
  between operations  0.76 us (2%)
    all_to_all x2, starting transfers between devices, exchange(): lax.all_to_all(x, 'ctx', split_axis=0, concat_axis=0, axis_index_groups=[...  24.2 us
    all_to_all x2, waiting for transfers between devices, exchange(): lax.all_to_all(x, 'ctx', split_axis=0, concat_axis=0, axis_index_groups=[...  9.16 us
    pallas_call x1, Pallas kernels, per_device(): pl.pallas_call(head_kernel, in_specs=[hbm, hbm, hbm], out_specs=hbm, out_...  2.9 us
    pallas_call x1, Pallas kernels, per_device(): pl.pallas_call(grad_filter_kernel, in_specs=[hbm, hbm, hbm, vmem, vmem, v...  2.85 us
    pallas_call x1, Pallas kernels, per_device(): pl.pallas_call(middle_kernel, in_specs=[vmem] * 7, out_specs=[hbm, vmem],...  2.5 us
    pallas_call x1, Pallas kernels, per_device(): pl.pallas_call(tail_kernel, in_specs=[vmem, vmem, vmem], out_specs=hbm, o...  1.48 us
  transfers between devices with their start and end apart: 2, of which 2 were waited for; matrix products, arithmetic and copies ran while one was open for 0% of the time, Pallas kernels for 8%

profile of v3, /device:TPU:0, one launch (start us, length us, event | category | flops | bytes accessed | tf_op | source)
XLA Modules:
  0.0 44.5 jit_solution(9263098179539715504)
XLA Ops:
  0.6 2.9 %head.1 = bf16[32,72,128]{2,1,0:T(8,128)(2,1)} custom-call(f32[3,3,4096]{2,1,0:T(4,128)} %taps_hbm.3, bf16[3,128,1024]{2,1,0:T(8,128)(2,1)} %br_hbm.3, bf16[128,1024]{1,0:T(8,128)(2,1)} %go_hbm.3), custom_call_target="tpu_custom_call" | custom-call | tf_op jit(solution)/shard_map/head/pallas_call | solution.py:407
  3.5 0.0 copy-start.1
  3.5 0.0 copy-start.2
  3.6 0.0 copy-start.4
  3.6 0.0 copy-start.5
  3.6 13.0 %all-to-all-start = ((bf16[32,72,128]{2,1,0:T(8,128)(2,1)}), bf16[32,72,128]{2,1,0:T(8,128)(2,1)S(1)}, u32[]{:S(2)}, u32[]{:S(2)}) async-start(bf16[32,72,128]{2,1,0:T(8,128)(2,1)} %head.1), calls=%async_computation | async-start | bytes 1179648 | tf_op jit(solution)/shard_map/all_to_all | solution.py:390
  16.6 0.0 copy-done.1
  16.6 0.0 copy-done.2
  16.6 0.0 copy-done.4
  16.6 0.0 copy-done.5
  16.6 0.0 copy-start
  16.6 0.0 copy-start.3
  16.6 0.5 %filter_spectrum.1.spec_ref = bf16[4,256,256]{2,1,0:T(8,128)(2,1)S(1)} custom-call(f32[32,4096]{1,0:T(8,128)S(1)} %copy-done.2, bf16[512,256]{1,0:T(8,128)(2,1)S(1)} %copy-done.1, bf16[256,256]{1,0:T(8,128)(2,1)S(1)} %copy-done.4, f32[2,32,128]{2,1,0:T(8,128)S(1)} %copy-done.5), custom_call_target="tpu_custom_call" | custom-call | tf_op jit(solution)/shard_map/filter_spectrum/pallas_call | solution.py:423
  17.2 6.4 %all-to-all-done.recv_ref = bf16[32,72,128]{2,1,0:T(8,128)(2,1)S(1)} async-done(((bf16[32,72,128]{2,1,0:T(8,128)(2,1)}), bf16[32,72,128]{2,1,0:T(8,128)(2,1)S(1)}, u32[]{:S(2)}, u32[]{:S(2)}) %all-to-all-start) | async-done | bytes 589856 | tf_op jit(solution)/shard_map/all_to_all | solution.py:390
  23.6 0.0 copy-done
  23.6 0.0 copy-done.3
  23.6 2.5 %middle.1 = (bf16[32,72,128]{2,1,0:T(8,128)(2,1)}, bf16[4,256,256]{2,1,0:T(8,128)(2,1)S(1)}) custom-call(bf16[32,72,128]{2,1,0:T(8,128)(2,1)S(1)} %all-to-all-done.recv_ref, bf16[4,256,256]{2,1,0:T(8,128)(2,1)S(1)} %filter_spectrum.1.spec_ref, bf16[512,256]{1,0:T(8,128)(2,1)S(1)} %copy-done.1, bf16[256,512]{1,0:T(8,128)(2,1)S(1)} %copy-done, ...), custom_call_target="tpu_custom_call" | custom-call | tf_op jit(solution)/shard_map/middle/pallas_call | solution.py:432
  26.1 11.3 %all-to-all-start.1 = ((bf16[32,72,128]{2,1,0:T(8,128)(2,1)}), bf16[32,72,128]{2,1,0:T(8,128)(2,1)S(1)}, u32[]{:S(2)}, u32[]{:S(2)}) async-start(bf16[32,72,128]{2,1,0:T(8,128)(2,1)} %get-tuple-element.10), calls=%async_computation.1 | async-start | bytes 1179648 | tf_op jit(solution)/shard_map/all_to_all | solution.py:390
  37.3 2.8 %grad_filter.1 = (f32[32,4096]{1,0:T(8,128)}, f32[3,3,1024]{2,1,0:T(4,128)S(1)}, bf16[3,128,1024]{2,1,0:T(8,128)(2,1)S(1)}) custom-call(f32[3,3,4096]{2,1,0:T(4,128)} %taps_hbm.3, bf16[3,128,1024]{2,1,0:T(8,128)(2,1)} %br_hbm.3, bf16[128,1024]{1,0:T(8,128)(2,1)} %go_hbm.3, bf16[4,256,256]{2,1,0:T(8,128)(2,1)S(1)} %get-tuple-element.7.corr_ref, ...), custom_call_target="tpu_custom_call" | custom-call | tf_op jit(solution)/shard_map/grad_filter/pallas_call | solution.py:441
  40.2 2.8 %all-to-all-done.1.recv_ref = bf16[32,72,128]{2,1,0:T(8,128)(2,1)S(1)} async-done(((bf16[32,72,128]{2,1,0:T(8,128)(2,1)}), bf16[32,72,128]{2,1,0:T(8,128)(2,1)S(1)}, u32[]{:S(2)}, u32[]{:S(2)}) %all-to-all-start.1) | async-done | bytes 589856 | tf_op jit(solution)/shard_map/all_to_all | solution.py:390
  43.0 1.5 %tail.1 = bf16[3,128,1024]{2,1,0:T(8,128)(2,1)} custom-call(f32[3,3,1024]{2,1,0:T(4,128)S(1)} %get-tuple-element.8.taps_ref, bf16[3,128,1024]{2,1,0:T(8,128)(2,1)S(1)} %get-tuple-element.9.rows_ref, bf16[32,72,128]{2,1,0:T(8,128)(2,1)S(1)} %all-to-all-done.1.recv_ref), custom_call_target="tpu_custom_call" | custom-call | tf_op jit(solution)/shard_map/tail/pallas_call | solution.py:458
Async XLA Ops:
  3.5 13.0 %copy-start.1 = (bf16[512,256]{1,0:T(8,128)(2,1)S(1)}, bf16[512,256]{1,0:T(8,128)(2,1)}, u32[]{:S(2)}) copy-start(bf16[512,256]{1,0:T(8,128)(2,1)} %constant.10.clone.lhs1_ref) | copy-start | bytes 786436
  3.5 13.0 %copy-start.2 = (f32[32,4096]{1,0:T(8,128)S(1)}, f32[32,4096]{1,0:T(8,128)}, u32[]{:S(2)}) copy-start(f32[32,4096]{1,0:T(8,128)} %filter_ref.1) | copy-start | bytes 1572868
  3.6 13.0 %copy-start.4 = (bf16[256,256]{1,0:T(8,128)(2,1)S(1)}, bf16[256,256]{1,0:T(8,128)(2,1)}, u32[]{:S(2)}) copy-start(bf16[256,256]{1,0:T(8,128)(2,1)} %constant.12.clone.fwd_ref) | copy-start | bytes 393220
  3.6 13.0 %copy-start.5 = (f32[2,32,128]{2,1,0:T(8,128)S(1)}, f32[2,32,128]{2,1,0:T(8,128)}, u32[]{:S(2)}) copy-start(f32[2,32,128]{2,1,0:T(8,128)} %constant.14.clone.twist_ref) | copy-start | bytes 98308
  3.6 20.0 %all-to-all-start = ((bf16[32,72,128]{2,1,0:T(8,128)(2,1)}), bf16[32,72,128]{2,1,0:T(8,128)(2,1)S(1)}, u32[]{:S(2)}, u32[]{:S(2)}) async-start(bf16[32,72,128]{2,1,0:T(8,128)(2,1)} %head.1), calls=%async_computation | async-start | bytes 1179648 | tf_op jit(solution)/shard_map/all_to_all | solution.py:390
  16.6 7.0 %copy-start = (bf16[256,512]{1,0:T(8,128)(2,1)S(1)}, bf16[256,512]{1,0:T(8,128)(2,1)}, u32[]{:S(2)}) copy-start(bf16[256,512]{1,0:T(8,128)(2,1)} %constant.11.clone.lhs2_ref) | copy-start | bytes 786436
  16.6 7.0 %copy-start.3 = (bf16[256,256]{1,0:T(8,128)(2,1)S(1)}, bf16[256,256]{1,0:T(8,128)(2,1)}, u32[]{:S(2)}) copy-start(bf16[256,256]{1,0:T(8,128)(2,1)} %constant.13.clone.inv_ref) | copy-start | bytes 393220
  26.1 16.9 %all-to-all-start.1 = ((bf16[32,72,128]{2,1,0:T(8,128)(2,1)}), bf16[32,72,128]{2,1,0:T(8,128)(2,1)S(1)}, u32[]{:S(2)}, u32[]{:S(2)}) async-start(bf16[32,72,128]{2,1,0:T(8,128)(2,1)} %get-tuple-element.10), calls=%async_computation.1 | async-start | bytes 1179648 | tf_op jit(solution)/shard_map/all_to_all | solution.py:390

commit v4 on v3

--- a/solution.py
+++ b/solution.py
@@ -19,6 +19,7 @@
 PERIOD = 2 * BLOCKS * CHUNK
 ROWS = 72
 CB = 256
+KB = 128
 
 
 def ctx_order():
@@ -87,67 +88,76 @@
     return jnp.concatenate([first, feat], axis=0), tail
 
 
-def head_block(taps_ref, rows_ref, send_ref, at):
-    cols = pl.ds(at, CB)
-    nd = CB // 32
-    row8 = lax.broadcasted_iota(jnp.int32, (8, CB), 0)
-    feats, tails = [], []
-    for b in range(3):
-        feat, tail = featurize(
-            rows_ref[b, :, cols].astype(F32), [taps_ref[b, j : j + 1, cols] for j in range(3)]
-        )
-        feats.append(feat)
-        tails.append(tail)
-    query, key, value = feats
+def head_feat(taps_ref, rows_ref, b, cols):
+    taps = [taps_ref[b, j : j + 1, cols] for j in range(3)]
+    return featurize(rows_ref[b, :, cols].astype(F32), taps)
+
+
+def head_store(send_ref, at, rows, value):
+    value = value.astype(BF16).T.reshape(KB // 32, 32, CHUNK)
+    for n in range(KB // 32):
+        send_ref[PLACE_IN[at // 32 + n], rows, :] = value[n]
+
+
+def head_products(taps_ref, rows_ref, terms_ref, send_ref, at):
+    cols = pl.ds(at, KB)
+    key, key_tail = head_feat(taps_ref, rows_ref, 1, cols)
+    value, value_tail = head_feat(taps_ref, rows_ref, 2, cols)
+    head_store(send_ref, at, slice(0, 32), key * value)
+    row8 = lax.broadcasted_iota(jnp.int32, (8, KB), 0)
+    for i, (k, v) in enumerate(((key[:8], value[:8]), (key_tail, value_tail))):
+        terms_ref[i, :, cols] = jnp.where(row8 < 4, pltpu.roll(k, 2, 0), pltpu.roll(v, 4, 0))
+
+
+def head_gate_grad(taps_ref, rows_ref, terms_ref, send_ref, at):
+    cols = pl.ds(at, KB)
+    query, query_tail = head_feat(taps_ref, rows_ref, 0, cols)
     go = rows_ref[3, :, cols].astype(F32)
-    products = (key * value).astype(BF16).T.reshape(nd, 32, CHUNK)
-    gate_grad = (go * query).astype(BF16).T.reshape(nd, 32, CHUNK)
-    heads = jnp.where(
-        row8 < 2,
-        query[:8],
-        jnp.where(
-            row8 < 4,
-            pltpu.roll(key[:8], 2, 0),
-            jnp.where(row8 < 6, pltpu.roll(value[:8], 4, 0), pltpu.roll(go[:8], 6, 0)),
-        ),
-    )
-    ends = jnp.where(
-        row8 < 2,
-        tails[0],
-        jnp.where(row8 < 4, pltpu.roll(tails[1], 2, 0), pltpu.roll(tails[2], 4, 0)),
-    )
-    quarter = lax.broadcasted_iota(jnp.int32, (8, CB), 1) // 8 % 4
+    head_store(send_ref, at, slice(32, 64), go * query)
+    row8 = lax.broadcasted_iota(jnp.int32, (8, KB), 0)
+    heads = jnp.where(row8 < 6, terms_ref[0, :, cols], pltpu.roll(go[:8], 6, 0))
+    heads = jnp.where(row8 < 2, query[:8], heads)
+    ends = jnp.where(row8 < 2, query_tail, terms_ref[1, :, cols])
+    quarter = lax.broadcasted_iota(jnp.int32, (8, KB), 1) // 8 % 4
     padded = []
     for q in range(4):
         padded += [jnp.where(quarter == q, heads, 0.0), jnp.where(quarter == q, ends, 0.0)]
-    padded.append(jnp.zeros((CHUNK - 64, CB), F32))
-    terms = jnp.concatenate(padded, axis=0).T.reshape(nd, 4, 8, CHUNK)
+    padded.append(jnp.zeros((CHUNK - 64, KB), F32))
+    terms = jnp.concatenate(padded, axis=0).T.reshape(KB // 32, 4, 8, CHUNK)
     terms = (terms[:, 0] + terms[:, 1] + terms[:, 2] + terms[:, 3]).astype(BF16)
-    for n in range(nd):
-        place = PLACE_IN[at // 32 + n]
-        send_ref[place, 0:32, :] = products[n]
-        send_ref[place, 32:64, :] = gate_grad[n]
-        send_ref[place, 64:72, :] = terms[n]
+    for n in range(KB // 32):
+        send_ref[PLACE_IN[at // 32 + n], 64:72, :] = terms[n]
 
 
 def head_kernel(
-    taps_hbm, br_hbm, go_hbm, send_hbm, taps_ref, rows_ref, send_ref, taps_sem, in_sem, out_sem
+    taps_hbm,
+    br_hbm,
+    go_hbm,
+    send_hbm,
+    taps_ref,
+    rows_ref,
+    terms_ref,
+    send_ref,
+    taps_sem,
+    in_sem,
+    out_sem,
 ):
     channels = rows_ref.shape[2]
-    nd = CB // 32
     taps_copy = pltpu.make_async_copy(taps_slice(taps_hbm, channels), taps_ref, taps_sem)
-    taps_copy.start()
-    blocks = [pl.ds(i * CB, CB) for i in range(channels // CB)]
-    for i, cols in enumerate(blocks):
-        dst = rows_ref.at[0:3, :, cols]
-        pltpu.make_async_copy(br_hbm.at[:, :, cols], dst, in_sem.at[i]).start()
-        pltpu.make_async_copy(go_hbm.at[:, cols], rows_ref.at[3, :, cols], in_sem.at[i]).start()
+    pair_copy = pltpu.make_async_copy(br_hbm.at[1:3], rows_ref.at[1:3], in_sem.at[0])
+    query_copy = pltpu.make_async_copy(br_hbm.at[0], rows_ref.at[0], in_sem.at[1])
+    go_copy = pltpu.make_async_copy(go_hbm, rows_ref.at[3], in_sem.at[2])
+    for copy in (taps_copy, pair_copy, query_copy, go_copy):
+        copy.start()
     taps_copy.wait()
-    for i, cols in enumerate(blocks):
-        both = rows_ref.at[:, :, cols]
-        pltpu.make_async_copy(both, both, in_sem.at[i]).wait()
-        head_block(taps_ref, rows_ref, send_ref, i * CB)
-        for first, length in runs(PLACE_IN[i * nd : (i + 1) * nd]):
+    pair_copy.wait()
+    for at in range(0, channels, KB):
+        head_products(taps_ref, rows_ref, terms_ref, send_ref, at)
+    query_copy.wait()
+    go_copy.wait()
+    for at in range(0, channels, KB):
+        head_gate_grad(taps_ref, rows_ref, terms_ref, send_ref, at)
+        for first, length in runs(PLACE_IN[at // 32 : (at + KB) // 32]):
             out = pl.ds(first, length)
             pltpu.make_async_copy(send_ref.at[out], send_hbm.at[out], out_sem).start()
     pltpu.make_async_copy(send_ref, send_hbm, out_sem).wait()
@@ -395,7 +405,6 @@
 def per_device(branches, short_taps, long_filter, grad_out):
     lhs1, lhs2, fwd, inv, twist = (jnp.asarray(t) for t in tables())
     tokens, channels = grad_out.shape
-    steps = channels // CB
     half = GROUP * HALF
     hbm = pl.BlockSpec(memory_space=pltpu.HBM)
     vmem = pl.BlockSpec(memory_space=pltpu.VMEM)
@@ -412,9 +421,10 @@
         scratch_shapes=[
             pltpu.VMEM((3, 3, channels), F32),
             pltpu.VMEM((4, tokens, channels), BF16),
+            pltpu.VMEM((2, 8, channels), F32),
             pltpu.VMEM(wire, BF16),
             dma,
-            dma((steps,)),
+            dma((3,)),
             dma,
         ],
         compiler_params=params(24),

time: 44.8 us -> 44.6 us (level)
  no operation moved by 1% of the time
where the time goes in v4:
time: 44.6 us; the launch traced here: 44.2 us
  starting transfers between devices  24.2 us (54%)
  Pallas kernels  10 us (22%)
  waiting for transfers between devices  9.16 us (21%)
  between operations  0.76 us (2%)
    all_to_all x2, starting transfers between devices, exchange(): lax.all_to_all(x, 'ctx', split_axis=0, concat_axis=0, axis_index_groups=[...  24.2 us
    all_to_all x2, waiting for transfers between devices, exchange(): lax.all_to_all(x, 'ctx', split_axis=0, concat_axis=0, axis_index_groups=[...  9.16 us
    pallas_call x1, Pallas kernels, per_device(): pl.pallas_call(grad_filter_kernel, in_specs=[hbm, hbm, hbm, vmem, vmem, v...  2.85 us
    pallas_call x1, Pallas kernels, per_device(): pl.pallas_call(head_kernel, in_specs=[hbm, hbm, hbm], out_specs=hbm, out_...  2.64 us
    pallas_call x1, Pallas kernels, per_device(): pl.pallas_call(middle_kernel, in_specs=[vmem] * 7, out_specs=[hbm, vmem],...  2.5 us
    pallas_call x1, Pallas kernels, per_device(): pl.pallas_call(tail_kernel, in_specs=[vmem, vmem, vmem], out_specs=hbm, o...  1.48 us
  transfers between devices with their start and end apart: 2, of which 2 were waited for; matrix products, arithmetic and copies ran while one was open for 0% of the time, Pallas kernels for 8%

profile of v4, /device:TPU:0, one launch (start us, length us, event | category | flops | bytes accessed | tf_op | source)
XLA Modules:
  0.0 44.2 jit_solution(17357173432456476049)
XLA Ops:
  0.6 2.6 %head.1 = bf16[32,72,128]{2,1,0:T(8,128)(2,1)} custom-call(f32[3,3,4096]{2,1,0:T(4,128)} %taps_hbm.3, bf16[3,128,1024]{2,1,0:T(8,128)(2,1)} %br_hbm.3, bf16[128,1024]{1,0:T(8,128)(2,1)} %go_hbm.3), custom_call_target="tpu_custom_call" | custom-call | tf_op jit(solution)/shard_map/head/pallas_call | solution.py:416
  3.3 0.0 copy-start.1
  3.3 0.0 copy-start.2
  3.3 0.0 copy-start.4
  3.3 0.0 copy-start.5
  3.3 13.0 %all-to-all-start = ((bf16[32,72,128]{2,1,0:T(8,128)(2,1)}), bf16[32,72,128]{2,1,0:T(8,128)(2,1)S(1)}, u32[]{:S(2)}, u32[]{:S(2)}) async-start(bf16[32,72,128]{2,1,0:T(8,128)(2,1)} %head.1), calls=%async_computation | async-start | bytes 1179648 | tf_op jit(solution)/shard_map/all_to_all | solution.py:400
  16.3 0.0 copy-done.1
  16.3 0.0 copy-done.2
  16.3 0.0 copy-done.4
  16.3 0.0 copy-done.5
  16.3 0.0 copy-start
  16.4 0.0 copy-start.3
  16.4 0.5 %filter_spectrum.1.spec_ref = bf16[4,256,256]{2,1,0:T(8,128)(2,1)S(1)} custom-call(f32[32,4096]{1,0:T(8,128)S(1)} %copy-done.2, bf16[512,256]{1,0:T(8,128)(2,1)S(1)} %copy-done.1, bf16[256,256]{1,0:T(8,128)(2,1)S(1)} %copy-done.4, f32[2,32,128]{2,1,0:T(8,128)S(1)} %copy-done.5), custom_call_target="tpu_custom_call" | custom-call | tf_op jit(solution)/shard_map/filter_spectrum/pallas_call | solution.py:433
  16.9 6.4 %all-to-all-done.recv_ref = bf16[32,72,128]{2,1,0:T(8,128)(2,1)S(1)} async-done(((bf16[32,72,128]{2,1,0:T(8,128)(2,1)}), bf16[32,72,128]{2,1,0:T(8,128)(2,1)S(1)}, u32[]{:S(2)}, u32[]{:S(2)}) %all-to-all-start) | async-done | bytes 589856 | tf_op jit(solution)/shard_map/all_to_all | solution.py:400
  23.3 0.0 copy-done
  23.3 0.0 copy-done.3
  23.3 2.5 %middle.1 = (bf16[32,72,128]{2,1,0:T(8,128)(2,1)}, bf16[4,256,256]{2,1,0:T(8,128)(2,1)S(1)}) custom-call(bf16[32,72,128]{2,1,0:T(8,128)(2,1)S(1)} %all-to-all-done.recv_ref, bf16[4,256,256]{2,1,0:T(8,128)(2,1)S(1)} %filter_spectrum.1.spec_ref, bf16[512,256]{1,0:T(8,128)(2,1)S(1)} %copy-done.1, bf16[256,512]{1,0:T(8,128)(2,1)S(1)} %copy-done, ...), custom_call_target="tpu_custom_call" | custom-call | tf_op jit(solution)/shard_map/middle/pallas_call | solution.py:442
  25.8 11.3 %all-to-all-start.1 = ((bf16[32,72,128]{2,1,0:T(8,128)(2,1)}), bf16[32,72,128]{2,1,0:T(8,128)(2,1)S(1)}, u32[]{:S(2)}, u32[]{:S(2)}) async-start(bf16[32,72,128]{2,1,0:T(8,128)(2,1)} %get-tuple-element.10), calls=%async_computation.1 | async-start | bytes 1179648 | tf_op jit(solution)/shard_map/all_to_all | solution.py:400
  37.1 2.8 %grad_filter.1 = (f32[32,4096]{1,0:T(8,128)}, f32[3,3,1024]{2,1,0:T(4,128)S(1)}, bf16[3,128,1024]{2,1,0:T(8,128)(2,1)S(1)}) custom-call(f32[3,3,4096]{2,1,0:T(4,128)} %taps_hbm.3, bf16[3,128,1024]{2,1,0:T(8,128)(2,1)} %br_hbm.3, bf16[128,1024]{1,0:T(8,128)(2,1)} %go_hbm.3, bf16[4,256,256]{2,1,0:T(8,128)(2,1)S(1)} %get-tuple-element.7.corr_ref, ...), custom_call_target="tpu_custom_call" | custom-call | tf_op jit(solution)/shard_map/grad_filter/pallas_call | solution.py:451
  39.9 2.8 %all-to-all-done.1.recv_ref = bf16[32,72,128]{2,1,0:T(8,128)(2,1)S(1)} async-done(((bf16[32,72,128]{2,1,0:T(8,128)(2,1)}), bf16[32,72,128]{2,1,0:T(8,128)(2,1)S(1)}, u32[]{:S(2)}, u32[]{:S(2)}) %all-to-all-start.1) | async-done | bytes 589856 | tf_op jit(solution)/shard_map/all_to_all | solution.py:400
  42.7 1.5 %tail.1 = bf16[3,128,1024]{2,1,0:T(8,128)(2,1)} custom-call(f32[3,3,1024]{2,1,0:T(4,128)S(1)} %get-tuple-element.8.taps_ref, bf16[3,128,1024]{2,1,0:T(8,128)(2,1)S(1)} %get-tuple-element.9.rows_ref, bf16[32,72,128]{2,1,0:T(8,128)(2,1)S(1)} %all-to-all-done.1.recv_ref), custom_call_target="tpu_custom_call" | custom-call | tf_op jit(solution)/shard_map/tail/pallas_call | solution.py:468
Async XLA Ops:
  3.3 13.0 %copy-start.1 = (bf16[512,256]{1,0:T(8,128)(2,1)S(1)}, bf16[512,256]{1,0:T(8,128)(2,1)}, u32[]{:S(2)}) copy-start(bf16[512,256]{1,0:T(8,128)(2,1)} %constant.10.clone.lhs1_ref) | copy-start | bytes 786436
  3.3 13.0 %copy-start.2 = (f32[32,4096]{1,0:T(8,128)S(1)}, f32[32,4096]{1,0:T(8,128)}, u32[]{:S(2)}) copy-start(f32[32,4096]{1,0:T(8,128)} %filter_ref.1) | copy-start | bytes 1572868
  3.3 13.0 %copy-start.4 = (bf16[256,256]{1,0:T(8,128)(2,1)S(1)}, bf16[256,256]{1,0:T(8,128)(2,1)}, u32[]{:S(2)}) copy-start(bf16[256,256]{1,0:T(8,128)(2,1)} %constant.12.clone.fwd_ref) | copy-start | bytes 393220
  3.3 13.0 %copy-start.5 = (f32[2,32,128]{2,1,0:T(8,128)S(1)}, f32[2,32,128]{2,1,0:T(8,128)}, u32[]{:S(2)}) copy-start(f32[2,32,128]{2,1,0:T(8,128)} %constant.14.clone.twist_ref) | copy-start | bytes 98308
  3.3 20.0 %all-to-all-start = ((bf16[32,72,128]{2,1,0:T(8,128)(2,1)}), bf16[32,72,128]{2,1,0:T(8,128)(2,1)S(1)}, u32[]{:S(2)}, u32[]{:S(2)}) async-start(bf16[32,72,128]{2,1,0:T(8,128)(2,1)} %head.1), calls=%async_computation | async-start | bytes 1179648 | tf_op jit(solution)/shard_map/all_to_all | solution.py:400
  16.3 7.0 %copy-start = (bf16[256,512]{1,0:T(8,128)(2,1)S(1)}, bf16[256,512]{1,0:T(8,128)(2,1)}, u32[]{:S(2)}) copy-start(bf16[256,512]{1,0:T(8,128)(2,1)} %constant.11.clone.lhs2_ref) | copy-start | bytes 786436
  16.4 7.0 %copy-start.3 = (bf16[256,256]{1,0:T(8,128)(2,1)S(1)}, bf16[256,256]{1,0:T(8,128)(2,1)}, u32[]{:S(2)}) copy-start(bf16[256,256]{1,0:T(8,128)(2,1)} %constant.13.clone.inv_ref) | copy-start | bytes 393220
  25.8 16.9 %all-to-all-start.1 = ((bf16[32,72,128]{2,1,0:T(8,128)(2,1)}), bf16[32,72,128]{2,1,0:T(8,128)(2,1)S(1)}, u32[]{:S(2)}, u32[]{:S(2)}) async-start(bf16[32,72,128]{2,1,0:T(8,128)(2,1)} %get-tuple-element.10), calls=%async_computation.1 | async-start | bytes 1179648 | tf_op jit(solution)/shard_map/all_to_all | solution.py:400

commit v5 on v4

--- a/solution.py
+++ b/solution.py
@@ -234,7 +234,7 @@
     send_hbm,
     corr_ref,
     send_ref,
-    sem,
+    sems,
 ):
     shape = (BLOCKS, GROUP, CHUNK)
     flat = (BLOCKS * GROUP, CHUNK)
@@ -286,7 +286,7 @@
             rows = slice(32 * i + 16 * j, 32 * i + 16 * (j + 1))
             send_ref[:, rows, :] = jnp.concatenate(outs[j][i], axis=1).astype(BF16)
             rows = pl.ds(32 * i + 16 * j, 16)
-            pltpu.make_async_copy(send_ref.at[:, rows], send_hbm.at[:, rows], sem).start()
+            pltpu.make_async_copy(send_ref.at[:, rows], send_hbm.at[:, rows], sems.at[0]).start()
     merged = []
     for i in range(2):
         merged.append(outs[0][i][0])
@@ -304,8 +304,11 @@
     terms = take(jnp.where(place < 8, feat, turn(after, 8)), ORDER_OUT)
     send_ref[:, 64:72, :] = terms.astype(BF16)
     rows = pl.ds(64, 8)
-    pltpu.make_async_copy(send_ref.at[:, rows], send_hbm.at[:, rows], sem).start()
-    pltpu.make_async_copy(send_ref, send_hbm, sem).wait()
+    last = pltpu.make_async_copy(send_ref.at[:, rows], send_hbm.at[:, rows], sems.at[1])
+    last.start()
+    rows = pl.ds(0, 64)
+    pltpu.make_async_copy(send_ref.at[:, rows], send_hbm.at[:, rows], sems.at[0]).wait()
+    last.wait()
 
 
 def grad_filter_kernel(
@@ -444,7 +447,7 @@
         in_specs=[vmem] * 7,
         out_specs=[hbm, vmem],
         out_shape=[pltpu.HBM(wire, BF16), pltpu.VMEM(spectral, BF16)],
-        scratch_shapes=[pltpu.VMEM(wire, BF16), dma],
+        scratch_shapes=[pltpu.VMEM(wire, BF16), dma((2,))],
         compiler_params=params(32),
         name="middle",
     )(recv, spectrum, lhs1, lhs2, fwd, inv, twist)

time: 44.6 us -> 44.6 us (level)
  no operation moved by 1% of the time
where the time goes in v5:
time: 44.6 us; the launch traced here: 44.2 us
  starting transfers between devices  24.2 us (54%)
  Pallas kernels  10 us (22%)
  waiting for transfers between devices  9.16 us (21%)
  between operations  0.76 us (2%)
    all_to_all x2, starting transfers between devices, exchange(): lax.all_to_all(x, 'ctx', split_axis=0, concat_axis=0, axis_index_groups=[...  24.2 us
    all_to_all x2, waiting for transfers between devices, exchange(): lax.all_to_all(x, 'ctx', split_axis=0, concat_axis=0, axis_index_groups=[...  9.16 us
    pallas_call x1, Pallas kernels, per_device(): pl.pallas_call(grad_filter_kernel, in_specs=[hbm, hbm, hbm, vmem, vmem, v...  2.85 us
    pallas_call x1, Pallas kernels, per_device(): pl.pallas_call(head_kernel, in_specs=[hbm, hbm, hbm], out_specs=hbm, out_...  2.64 us
    pallas_call x1, Pallas kernels, per_device(): pl.pallas_call(middle_kernel, in_specs=[vmem] * 7, out_specs=[hbm, vmem],...  2.51 us
    pallas_call x1, Pallas kernels, per_device(): pl.pallas_call(tail_kernel, in_specs=[vmem, vmem, vmem], out_specs=hbm, o...  1.48 us
  transfers between devices with their start and end apart: 2, of which 2 were waited for; matrix products, arithmetic and copies ran while one was open for 0% of the time, Pallas kernels for 8%

profile of v5, /device:TPU:0, one launch (start us, length us, event | category | flops | bytes accessed | tf_op | source)
XLA Modules:
  0.0 44.2 jit_solution(13767116442101244582)
XLA Ops:
  0.6 2.6 %head.1 = bf16[32,72,128]{2,1,0:T(8,128)(2,1)} custom-call(f32[3,3,4096]{2,1,0:T(4,128)} %taps_hbm.3, bf16[3,128,1024]{2,1,0:T(8,128)(2,1)} %br_hbm.3, bf16[128,1024]{1,0:T(8,128)(2,1)} %go_hbm.3), custom_call_target="tpu_custom_call" | custom-call | tf_op jit(solution)/shard_map/head/pallas_call | solution.py:419
  3.3 0.0 copy-start.1
  3.3 0.0 copy-start.2
  3.3 0.0 copy-start.4
  3.3 0.0 copy-start.5
  3.3 13.0 %all-to-all-start = ((bf16[32,72,128]{2,1,0:T(8,128)(2,1)}), bf16[32,72,128]{2,1,0:T(8,128)(2,1)S(1)}, u32[]{:S(2)}, u32[]{:S(2)}) async-start(bf16[32,72,128]{2,1,0:T(8,128)(2,1)} %head.1), calls=%async_computation | async-start | bytes 1179648 | tf_op jit(solution)/shard_map/all_to_all | solution.py:403
  16.3 0.0 copy-done.1
  16.3 0.0 copy-done.2
  16.3 0.0 copy-done.4
  16.3 0.0 copy-done.5
  16.3 0.0 copy-start
  16.4 0.0 copy-start.3
  16.4 0.5 %filter_spectrum.1.spec_ref = bf16[4,256,256]{2,1,0:T(8,128)(2,1)S(1)} custom-call(f32[32,4096]{1,0:T(8,128)S(1)} %copy-done.2, bf16[512,256]{1,0:T(8,128)(2,1)S(1)} %copy-done.1, bf16[256,256]{1,0:T(8,128)(2,1)S(1)} %copy-done.4, f32[2,32,128]{2,1,0:T(8,128)S(1)} %copy-done.5), custom_call_target="tpu_custom_call" | custom-call | tf_op jit(solution)/shard_map/filter_spectrum/pallas_call | solution.py:436
  16.9 6.4 %all-to-all-done.recv_ref = bf16[32,72,128]{2,1,0:T(8,128)(2,1)S(1)} async-done(((bf16[32,72,128]{2,1,0:T(8,128)(2,1)}), bf16[32,72,128]{2,1,0:T(8,128)(2,1)S(1)}, u32[]{:S(2)}, u32[]{:S(2)}) %all-to-all-start) | async-done | bytes 589856 | tf_op jit(solution)/shard_map/all_to_all | solution.py:403
  23.3 0.0 copy-done
  23.3 0.0 copy-done.3
  23.3 2.5 %middle.1 = (bf16[32,72,128]{2,1,0:T(8,128)(2,1)}, bf16[4,256,256]{2,1,0:T(8,128)(2,1)S(1)}) custom-call(bf16[32,72,128]{2,1,0:T(8,128)(2,1)S(1)} %all-to-all-done.recv_ref, bf16[4,256,256]{2,1,0:T(8,128)(2,1)S(1)} %filter_spectrum.1.spec_ref, bf16[512,256]{1,0:T(8,128)(2,1)S(1)} %copy-done.1, bf16[256,512]{1,0:T(8,128)(2,1)S(1)} %copy-done, ...), custom_call_target="tpu_custom_call" | custom-call | tf_op jit(solution)/shard_map/middle/pallas_call | solution.py:445
  25.8 11.3 %all-to-all-start.1 = ((bf16[32,72,128]{2,1,0:T(8,128)(2,1)}), bf16[32,72,128]{2,1,0:T(8,128)(2,1)S(1)}, u32[]{:S(2)}, u32[]{:S(2)}) async-start(bf16[32,72,128]{2,1,0:T(8,128)(2,1)} %get-tuple-element.10), calls=%async_computation.1 | async-start | bytes 1179648 | tf_op jit(solution)/shard_map/all_to_all | solution.py:403
  37.1 2.8 %grad_filter.1 = (f32[32,4096]{1,0:T(8,128)}, f32[3,3,1024]{2,1,0:T(4,128)S(1)}, bf16[3,128,1024]{2,1,0:T(8,128)(2,1)S(1)}) custom-call(f32[3,3,4096]{2,1,0:T(4,128)} %taps_hbm.3, bf16[3,128,1024]{2,1,0:T(8,128)(2,1)} %br_hbm.3, bf16[128,1024]{1,0:T(8,128)(2,1)} %go_hbm.3, bf16[4,256,256]{2,1,0:T(8,128)(2,1)S(1)} %get-tuple-element.7.corr_ref, ...), custom_call_target="tpu_custom_call" | custom-call | tf_op jit(solution)/shard_map/grad_filter/pallas_call | solution.py:454
  40.0 2.8 %all-to-all-done.1.recv_ref = bf16[32,72,128]{2,1,0:T(8,128)(2,1)S(1)} async-done(((bf16[32,72,128]{2,1,0:T(8,128)(2,1)}), bf16[32,72,128]{2,1,0:T(8,128)(2,1)S(1)}, u32[]{:S(2)}, u32[]{:S(2)}) %all-to-all-start.1) | async-done | bytes 589856 | tf_op jit(solution)/shard_map/all_to_all | solution.py:403
  42.7 1.5 %tail.1 = bf16[3,128,1024]{2,1,0:T(8,128)(2,1)} custom-call(f32[3,3,1024]{2,1,0:T(4,128)S(1)} %get-tuple-element.8.taps_ref, bf16[3,128,1024]{2,1,0:T(8,128)(2,1)S(1)} %get-tuple-element.9.rows_ref, bf16[32,72,128]{2,1,0:T(8,128)(2,1)S(1)} %all-to-all-done.1.recv_ref), custom_call_target="tpu_custom_call" | custom-call | tf_op jit(solution)/shard_map/tail/pallas_call | solution.py:471
Async XLA Ops:
  3.3 13.0 %copy-start.1 = (bf16[512,256]{1,0:T(8,128)(2,1)S(1)}, bf16[512,256]{1,0:T(8,128)(2,1)}, u32[]{:S(2)}) copy-start(bf16[512,256]{1,0:T(8,128)(2,1)} %constant.10.clone.lhs1_ref) | copy-start | bytes 786436
  3.3 13.0 %copy-start.2 = (f32[32,4096]{1,0:T(8,128)S(1)}, f32[32,4096]{1,0:T(8,128)}, u32[]{:S(2)}) copy-start(f32[32,4096]{1,0:T(8,128)} %filter_ref.1) | copy-start | bytes 1572868
  3.3 13.0 %copy-start.4 = (bf16[256,256]{1,0:T(8,128)(2,1)S(1)}, bf16[256,256]{1,0:T(8,128)(2,1)}, u32[]{:S(2)}) copy-start(bf16[256,256]{1,0:T(8,128)(2,1)} %constant.12.clone.fwd_ref) | copy-start | bytes 393220
  3.3 13.0 %copy-start.5 = (f32[2,32,128]{2,1,0:T(8,128)S(1)}, f32[2,32,128]{2,1,0:T(8,128)}, u32[]{:S(2)}) copy-start(f32[2,32,128]{2,1,0:T(8,128)} %constant.14.clone.twist_ref) | copy-start | bytes 98308
  3.3 20.0 %all-to-all-start = ((bf16[32,72,128]{2,1,0:T(8,128)(2,1)}), bf16[32,72,128]{2,1,0:T(8,128)(2,1)S(1)}, u32[]{:S(2)}, u32[]{:S(2)}) async-start(bf16[32,72,128]{2,1,0:T(8,128)(2,1)} %head.1), calls=%async_computation | async-start | bytes 1179648 | tf_op jit(solution)/shard_map/all_to_all | solution.py:403
  16.3 7.0 %copy-start = (bf16[256,512]{1,0:T(8,128)(2,1)S(1)}, bf16[256,512]{1,0:T(8,128)(2,1)}, u32[]{:S(2)}) copy-start(bf16[256,512]{1,0:T(8,128)(2,1)} %constant.11.clone.lhs2_ref) | copy-start | bytes 786436
  16.4 7.0 %copy-start.3 = (bf16[256,256]{1,0:T(8,128)(2,1)S(1)}, bf16[256,256]{1,0:T(8,128)(2,1)}, u32[]{:S(2)}) copy-start(bf16[256,256]{1,0:T(8,128)(2,1)} %constant.13.clone.inv_ref) | copy-start | bytes 393220
  25.8 16.9 %all-to-all-start.1 = ((bf16[32,72,128]{2,1,0:T(8,128)(2,1)}), bf16[32,72,128]{2,1,0:T(8,128)(2,1)S(1)}, u32[]{:S(2)}, u32[]{:S(2)}) async-start(bf16[32,72,128]{2,1,0:T(8,128)(2,1)} %get-tuple-element.10), calls=%async_computation.1 | async-start | bytes 1179648 | tf_op jit(solution)/shard_map/all_to_all | solution.py:403

commit v6 on v5

--- a/solution.py
+++ b/solution.py
@@ -19,16 +19,17 @@
 PERIOD = 2 * BLOCKS * CHUNK
 ROWS = 72
 CB = 256
+TAIL_PARTS = (3, 2, 2, 1)
 KB = 128
 
 
-def ctx_order():
-    lexical = [8 * z + 2 * y + x for y in range(4) for x in range(2) for z in range(4)]
+def ctx_order(turn):
+    lexical = [8 * z + 2 * (turn * y % 4) + x for y in range(4) for x in range(2) for z in range(4)]
     return [lexical[13 * j % BLOCKS] ^ 21 for j in range(BLOCKS)]
 
 
-ORDER_IN = ctx_order()
-ORDER_OUT = ctx_order()
+ORDER_IN = ctx_order(1)
+ORDER_OUT = ctx_order(-1)
 PLACE_IN = [ORDER_IN.index(i) for i in range(BLOCKS)]
 PLACE_OUT = [ORDER_OUT.index(i) for i in range(BLOCKS)]
 
@@ -283,10 +284,10 @@
             dzetas.append(value[:, CHUNK:].reshape(shape))
         outs.append((convs, dzetas))
         for i in range(2):
-            rows = slice(32 * i + 16 * j, 32 * i + 16 * (j + 1))
+            rows = slice(32 * j + 16 * i, 32 * j + 16 * (i + 1))
             send_ref[:, rows, :] = jnp.concatenate(outs[j][i], axis=1).astype(BF16)
-            rows = pl.ds(32 * i + 16 * j, 16)
-            pltpu.make_async_copy(send_ref.at[:, rows], send_hbm.at[:, rows], sems.at[0]).start()
+        rows = pl.ds(32 * j, 32)
+        pltpu.make_async_copy(send_ref.at[:, rows], send_hbm.at[:, rows], sems.at[0]).start()
     merged = []
     for i in range(2):
         merged.append(outs[0][i][0])
@@ -355,16 +356,17 @@
                 )
 
 
-def tail_block(taps_ref, rows_ref, recv_ref, out_ref, at):
-    cols = pl.ds(at, CB)
-    row8 = lax.broadcasted_iota(jnp.int32, (8, CB), 0)
-    places = PLACE_OUT[at // 32 : (at + CB) // 32]
-    received = lambda rows: jnp.stack([recv_ref[p, rows, :] for p in places])
-    conv = received(slice(0, 32)).reshape(CB, CHUNK).T.astype(F32)
-    dzeta = received(slice(32, 64)).reshape(CB, CHUNK).T.astype(F32)
-    halo = received(slice(64, 72)).astype(F32)
+def tail_block(taps_ref, rows_ref, recv_ref, out_ref, at, size):
+    cols = pl.ds(at, size)
+    row8 = lax.broadcasted_iota(jnp.int32, (8, size), 0)
+    places = PLACE_OUT[at // 32 : (at + size) // 32]
+    conv = [recv_ref[p, i : i + 16, :] for p in places for i in (0, 32)]
+    dzeta = [recv_ref[p, i : i + 16, :] for p in places for i in (16, 48)]
+    conv = jnp.concatenate(conv, axis=0).T.astype(F32)
+    dzeta = jnp.concatenate(dzeta, axis=0).T.astype(F32)
+    halo = jnp.stack([recv_ref[p, 64:72, :] for p in places]).astype(F32)
     turned = [halo] + [pltpu.roll(halo, CHUNK - SLOT * q, 2) for q in range(1, 4)]
-    halo = jnp.concatenate(turned, axis=1).reshape(CB, CHUNK).T
+    halo = jnp.concatenate(turned, axis=1).reshape(size, CHUNK).T
     heads, nexts = halo[:8], halo[8:16]
 
     def with_head(b, at):
@@ -388,10 +390,13 @@
 
 
 def tail_kernel(taps_ref, rows_ref, recv_ref, out_hbm, out_ref, sem):
-    for i in range(out_ref.shape[2] // CB):
-        tail_block(taps_ref, rows_ref, recv_ref, out_ref, i * CB)
-        cols = pl.ds(i * CB, CB)
+    at = 0
+    for part in TAIL_PARTS:
+        size = out_ref.shape[2] * part // 8
+        tail_block(taps_ref, rows_ref, recv_ref, out_ref, at, size)
+        cols = pl.ds(at, size)
         pltpu.make_async_copy(out_ref.at[:, :, cols], out_hbm.at[:, :, cols], sem).start()
+        at += size
     pltpu.make_async_copy(out_ref, out_hbm, sem).wait()
 
 

time: 44.6 us -> 44.5 us (level)
  no operation moved by 1% of the time
where the time goes in v6:
time: 44.5 us; the launch traced here: 44.2 us
  starting transfers between devices  24.2 us (54%)
  Pallas kernels  9.99 us (22%)
  waiting for transfers between devices  9.16 us (21%)
  between operations  0.76 us (2%)
    all_to_all x2, starting transfers between devices, exchange(): lax.all_to_all(x, 'ctx', split_axis=0, concat_axis=0, axis_index_groups=[...  24.2 us
    all_to_all x2, waiting for transfers between devices, exchange(): lax.all_to_all(x, 'ctx', split_axis=0, concat_axis=0, axis_index_groups=[...  9.16 us
    pallas_call x1, Pallas kernels, per_device(): pl.pallas_call(grad_filter_kernel, in_specs=[hbm, hbm, hbm, vmem, vmem, v...  2.85 us
    pallas_call x1, Pallas kernels, per_device(): pl.pallas_call(head_kernel, in_specs=[hbm, hbm, hbm], out_specs=hbm, out_...  2.64 us
    pallas_call x1, Pallas kernels, per_device(): pl.pallas_call(middle_kernel, in_specs=[vmem] * 7, out_specs=[hbm, vmem],...  2.49 us
    pallas_call x1, Pallas kernels, per_device(): pl.pallas_call(tail_kernel, in_specs=[vmem, vmem, vmem], out_specs=hbm, o...  1.46 us
  transfers between devices with their start and end apart: 2, of which 2 were waited for; matrix products, arithmetic and copies ran while one was open for 0% of the time, Pallas kernels for 8%

profile of v6, /device:TPU:0, one launch (start us, length us, event | category | flops | bytes accessed | tf_op | source)
XLA Modules:
  0.0 44.2 jit_solution(1359760149896234375)
XLA Ops:
  0.6 2.6 %head.1 = bf16[32,72,128]{2,1,0:T(8,128)(2,1)} custom-call(f32[3,3,4096]{2,1,0:T(4,128)} %taps_hbm.3, bf16[3,128,1024]{2,1,0:T(8,128)(2,1)} %br_hbm.3, bf16[128,1024]{1,0:T(8,128)(2,1)} %go_hbm.3), custom_call_target="tpu_custom_call" | custom-call | tf_op jit(solution)/shard_map/head/pallas_call | solution.py:424
  3.3 0.0 copy-start.1
  3.3 0.0 copy-start.2
  3.3 0.0 copy-start.4
  3.3 0.0 copy-start.5
  3.3 13.0 %all-to-all-start = ((bf16[32,72,128]{2,1,0:T(8,128)(2,1)}), bf16[32,72,128]{2,1,0:T(8,128)(2,1)S(1)}, u32[]{:S(2)}, u32[]{:S(2)}) async-start(bf16[32,72,128]{2,1,0:T(8,128)(2,1)} %head.1), calls=%async_computation | async-start | bytes 1179648 | tf_op jit(solution)/shard_map/all_to_all | solution.py:408
  16.3 0.0 copy-done.1
  16.3 0.0 copy-done.2
  16.3 0.0 copy-done.4
  16.3 0.0 copy-done.5
  16.3 0.0 copy-start
  16.4 0.0 copy-start.3
  16.4 0.5 %filter_spectrum.1.spec_ref = bf16[4,256,256]{2,1,0:T(8,128)(2,1)S(1)} custom-call(f32[32,4096]{1,0:T(8,128)S(1)} %copy-done.2, bf16[512,256]{1,0:T(8,128)(2,1)S(1)} %copy-done.1, bf16[256,256]{1,0:T(8,128)(2,1)S(1)} %copy-done.4, f32[2,32,128]{2,1,0:T(8,128)S(1)} %copy-done.5), custom_call_target="tpu_custom_call" | custom-call | tf_op jit(solution)/shard_map/filter_spectrum/pallas_call | solution.py:441
  16.9 6.4 %all-to-all-done.recv_ref = bf16[32,72,128]{2,1,0:T(8,128)(2,1)S(1)} async-done(((bf16[32,72,128]{2,1,0:T(8,128)(2,1)}), bf16[32,72,128]{2,1,0:T(8,128)(2,1)S(1)}, u32[]{:S(2)}, u32[]{:S(2)}) %all-to-all-start) | async-done | bytes 589856 | tf_op jit(solution)/shard_map/all_to_all | solution.py:408
  23.3 0.0 copy-done
  23.3 0.0 copy-done.3
  23.3 2.5 %middle.1 = (bf16[32,72,128]{2,1,0:T(8,128)(2,1)}, bf16[4,256,256]{2,1,0:T(8,128)(2,1)S(1)}) custom-call(bf16[32,72,128]{2,1,0:T(8,128)(2,1)S(1)} %all-to-all-done.recv_ref, bf16[4,256,256]{2,1,0:T(8,128)(2,1)S(1)} %filter_spectrum.1.spec_ref, bf16[512,256]{1,0:T(8,128)(2,1)S(1)} %copy-done.1, bf16[256,512]{1,0:T(8,128)(2,1)S(1)} %copy-done, ...), custom_call_target="tpu_custom_call" | custom-call | tf_op jit(solution)/shard_map/middle/pallas_call | solution.py:450
  25.8 11.3 %all-to-all-start.1 = ((bf16[32,72,128]{2,1,0:T(8,128)(2,1)}), bf16[32,72,128]{2,1,0:T(8,128)(2,1)S(1)}, u32[]{:S(2)}, u32[]{:S(2)}) async-start(bf16[32,72,128]{2,1,0:T(8,128)(2,1)} %get-tuple-element.10), calls=%async_computation.1 | async-start | bytes 1179648 | tf_op jit(solution)/shard_map/all_to_all | solution.py:408
  37.1 2.8 %grad_filter.1 = (f32[32,4096]{1,0:T(8,128)}, f32[3,3,1024]{2,1,0:T(4,128)S(1)}, bf16[3,128,1024]{2,1,0:T(8,128)(2,1)S(1)}) custom-call(f32[3,3,4096]{2,1,0:T(4,128)} %taps_hbm.3, bf16[3,128,1024]{2,1,0:T(8,128)(2,1)} %br_hbm.3, bf16[128,1024]{1,0:T(8,128)(2,1)} %go_hbm.3, bf16[4,256,256]{2,1,0:T(8,128)(2,1)S(1)} %get-tuple-element.7.corr_ref, ...), custom_call_target="tpu_custom_call" | custom-call | tf_op jit(solution)/shard_map/grad_filter/pallas_call | solution.py:459
  39.9 2.8 %all-to-all-done.1.recv_ref = bf16[32,72,128]{2,1,0:T(8,128)(2,1)S(1)} async-done(((bf16[32,72,128]{2,1,0:T(8,128)(2,1)}), bf16[32,72,128]{2,1,0:T(8,128)(2,1)S(1)}, u32[]{:S(2)}, u32[]{:S(2)}) %all-to-all-start.1) | async-done | bytes 589856 | tf_op jit(solution)/shard_map/all_to_all | solution.py:408
  42.7 1.5 %tail.1 = bf16[3,128,1024]{2,1,0:T(8,128)(2,1)} custom-call(f32[3,3,1024]{2,1,0:T(4,128)S(1)} %get-tuple-element.8.taps_ref, bf16[3,128,1024]{2,1,0:T(8,128)(2,1)S(1)} %get-tuple-element.9.rows_ref, bf16[32,72,128]{2,1,0:T(8,128)(2,1)S(1)} %all-to-all-done.1.recv_ref), custom_call_target="tpu_custom_call" | custom-call | tf_op jit(solution)/shard_map/tail/pallas_call | solution.py:476
Async XLA Ops:
  3.3 13.0 %copy-start.1 = (bf16[512,256]{1,0:T(8,128)(2,1)S(1)}, bf16[512,256]{1,0:T(8,128)(2,1)}, u32[]{:S(2)}) copy-start(bf16[512,256]{1,0:T(8,128)(2,1)} %constant.10.clone.lhs1_ref) | copy-start | bytes 786436
  3.3 13.0 %copy-start.2 = (f32[32,4096]{1,0:T(8,128)S(1)}, f32[32,4096]{1,0:T(8,128)}, u32[]{:S(2)}) copy-start(f32[32,4096]{1,0:T(8,128)} %filter_ref.1) | copy-start | bytes 1572868
  3.3 13.0 %copy-start.4 = (bf16[256,256]{1,0:T(8,128)(2,1)S(1)}, bf16[256,256]{1,0:T(8,128)(2,1)}, u32[]{:S(2)}) copy-start(bf16[256,256]{1,0:T(8,128)(2,1)} %constant.12.clone.fwd_ref) | copy-start | bytes 393220
  3.3 13.0 %copy-start.5 = (f32[2,32,128]{2,1,0:T(8,128)S(1)}, f32[2,32,128]{2,1,0:T(8,128)}, u32[]{:S(2)}) copy-start(f32[2,32,128]{2,1,0:T(8,128)} %constant.14.clone.twist_ref) | copy-start | bytes 98308
  3.3 20.0 %all-to-all-start = ((bf16[32,72,128]{2,1,0:T(8,128)(2,1)}), bf16[32,72,128]{2,1,0:T(8,128)(2,1)S(1)}, u32[]{:S(2)}, u32[]{:S(2)}) async-start(bf16[32,72,128]{2,1,0:T(8,128)(2,1)} %head.1), calls=%async_computation | async-start | bytes 1179648 | tf_op jit(solution)/shard_map/all_to_all | solution.py:408
  16.3 7.0 %copy-start = (bf16[256,512]{1,0:T(8,128)(2,1)S(1)}, bf16[256,512]{1,0:T(8,128)(2,1)}, u32[]{:S(2)}) copy-start(bf16[256,512]{1,0:T(8,128)(2,1)} %constant.11.clone.lhs2_ref) | copy-start | bytes 786436
  16.4 7.0 %copy-start.3 = (bf16[256,256]{1,0:T(8,128)(2,1)S(1)}, bf16[256,256]{1,0:T(8,128)(2,1)}, u32[]{:S(2)}) copy-start(bf16[256,256]{1,0:T(8,128)(2,1)} %constant.13.clone.inv_ref) | copy-start | bytes 393220
  25.8 16.9 %all-to-all-start.1 = ((bf16[32,72,128]{2,1,0:T(8,128)(2,1)}), bf16[32,72,128]{2,1,0:T(8,128)(2,1)S(1)}, u32[]{:S(2)}, u32[]{:S(2)}) async-start(bf16[32,72,128]{2,1,0:T(8,128)(2,1)} %get-tuple-element.10), calls=%async_computation.1 | async-start | bytes 1179648 | tf_op jit(solution)/shard_map/all_to_all | solution.py:408

commit v7 on v6

--- a/solution.py
+++ b/solution.py
@@ -154,14 +154,19 @@
     pair_copy.wait()
     for at in range(0, channels, KB):
         head_products(taps_ref, rows_ref, terms_ref, send_ref, at)
+    done = pl.ds(0, 32)
+    early = pltpu.make_async_copy(send_ref.at[:, done], send_hbm.at[:, done], in_sem.at[0])
+    early.start()
+    rest = pl.ds(32, ROWS - 32)
     query_copy.wait()
     go_copy.wait()
     for at in range(0, channels, KB):
         head_gate_grad(taps_ref, rows_ref, terms_ref, send_ref, at)
         for first, length in runs(PLACE_IN[at // 32 : (at + KB) // 32]):
             out = pl.ds(first, length)
-            pltpu.make_async_copy(send_ref.at[out], send_hbm.at[out], out_sem).start()
-    pltpu.make_async_copy(send_ref, send_hbm, out_sem).wait()
+            pltpu.make_async_copy(send_ref.at[out, rest], send_hbm.at[out, rest], out_sem).start()
+    early.wait()
+    pltpu.make_async_copy(send_ref.at[:, rest], send_hbm.at[:, rest], out_sem).wait()
 
 
 def spread(signals, lhs1_ref, twist_ref):

time: 44.5 us -> 44.5 us (level)
  no operation moved by 1% of the time
where the time goes in v7:
time: 44.5 us; the launch traced here: 44.2 us
  starting transfers between devices  24.2 us (54%)
  Pallas kernels  9.97 us (22%)
  waiting for transfers between devices  9.16 us (21%)
  between operations  0.76 us (2%)
    all_to_all x2, starting transfers between devices, exchange(): lax.all_to_all(x, 'ctx', split_axis=0, concat_axis=0, axis_index_groups=[...  24.2 us
    all_to_all x2, waiting for transfers between devices, exchange(): lax.all_to_all(x, 'ctx', split_axis=0, concat_axis=0, axis_index_groups=[...  9.16 us
    pallas_call x1, Pallas kernels, per_device(): pl.pallas_call(grad_filter_kernel, in_specs=[hbm, hbm, hbm, vmem, vmem, v...  2.85 us
    pallas_call x1, Pallas kernels, per_device(): pl.pallas_call(head_kernel, in_specs=[hbm, hbm, hbm], out_specs=hbm, out_...  2.63 us
    pallas_call x1, Pallas kernels, per_device(): pl.pallas_call(middle_kernel, in_specs=[vmem] * 7, out_specs=[hbm, vmem],...  2.49 us
    pallas_call x1, Pallas kernels, per_device(): pl.pallas_call(tail_kernel, in_specs=[vmem, vmem, vmem], out_specs=hbm, o...  1.46 us
  transfers between devices with their start and end apart: 2, of which 2 were waited for; matrix products, arithmetic and copies ran while one was open for 0% of the time, Pallas kernels for 8%

profile of v7, /device:TPU:0, one launch (start us, length us, event | category | flops | bytes accessed | tf_op | source)
XLA Modules:
  0.0 44.2 jit_solution(11882841922569273490)
XLA Ops:
  0.6 2.6 %head.1 = bf16[32,72,128]{2,1,0:T(8,128)(2,1)} custom-call(f32[3,3,4096]{2,1,0:T(4,128)} %taps_hbm.3, bf16[3,128,1024]{2,1,0:T(8,128)(2,1)} %br_hbm.3, bf16[128,1024]{1,0:T(8,128)(2,1)} %go_hbm.3), custom_call_target="tpu_custom_call" | custom-call | tf_op jit(solution)/shard_map/head/pallas_call | solution.py:429
  3.3 0.0 copy-start.1
  3.3 0.0 copy-start.2
  3.3 0.0 copy-start.4
  3.3 0.0 copy-start.5
  3.3 13.0 %all-to-all-start = ((bf16[32,72,128]{2,1,0:T(8,128)(2,1)}), bf16[32,72,128]{2,1,0:T(8,128)(2,1)S(1)}, u32[]{:S(2)}, u32[]{:S(2)}) async-start(bf16[32,72,128]{2,1,0:T(8,128)(2,1)} %head.1), calls=%async_computation | async-start | bytes 1179648 | tf_op jit(solution)/shard_map/all_to_all | solution.py:413
  16.3 0.0 copy-done.1
  16.3 0.0 copy-done.2
  16.3 0.0 copy-done.4
  16.3 0.0 copy-done.5
  16.3 0.0 copy-start
  16.3 0.0 copy-start.3
  16.4 0.6 %filter_spectrum.1.spec_ref = bf16[4,256,256]{2,1,0:T(8,128)(2,1)S(1)} custom-call(f32[32,4096]{1,0:T(8,128)S(1)} %copy-done.2, bf16[512,256]{1,0:T(8,128)(2,1)S(1)} %copy-done.1, bf16[256,256]{1,0:T(8,128)(2,1)S(1)} %copy-done.4, f32[2,32,128]{2,1,0:T(8,128)S(1)} %copy-done.5), custom_call_target="tpu_custom_call" | custom-call | tf_op jit(solution)/shard_map/filter_spectrum/pallas_call | solution.py:446
  16.9 6.4 %all-to-all-done.recv_ref = bf16[32,72,128]{2,1,0:T(8,128)(2,1)S(1)} async-done(((bf16[32,72,128]{2,1,0:T(8,128)(2,1)}), bf16[32,72,128]{2,1,0:T(8,128)(2,1)S(1)}, u32[]{:S(2)}, u32[]{:S(2)}) %all-to-all-start) | async-done | bytes 589856 | tf_op jit(solution)/shard_map/all_to_all | solution.py:413
  23.3 0.0 copy-done
  23.3 0.0 copy-done.3
  23.3 2.5 %middle.1 = (bf16[32,72,128]{2,1,0:T(8,128)(2,1)}, bf16[4,256,256]{2,1,0:T(8,128)(2,1)S(1)}) custom-call(bf16[32,72,128]{2,1,0:T(8,128)(2,1)S(1)} %all-to-all-done.recv_ref, bf16[4,256,256]{2,1,0:T(8,128)(2,1)S(1)} %filter_spectrum.1.spec_ref, bf16[512,256]{1,0:T(8,128)(2,1)S(1)} %copy-done.1, bf16[256,512]{1,0:T(8,128)(2,1)S(1)} %copy-done, ...), custom_call_target="tpu_custom_call" | custom-call | tf_op jit(solution)/shard_map/middle/pallas_call | solution.py:455
  25.8 11.3 %all-to-all-start.1 = ((bf16[32,72,128]{2,1,0:T(8,128)(2,1)}), bf16[32,72,128]{2,1,0:T(8,128)(2,1)S(1)}, u32[]{:S(2)}, u32[]{:S(2)}) async-start(bf16[32,72,128]{2,1,0:T(8,128)(2,1)} %get-tuple-element.10), calls=%async_computation.1 | async-start | bytes 1179648 | tf_op jit(solution)/shard_map/all_to_all | solution.py:413
  37.1 2.8 %grad_filter.1 = (f32[32,4096]{1,0:T(8,128)}, f32[3,3,1024]{2,1,0:T(4,128)S(1)}, bf16[3,128,1024]{2,1,0:T(8,128)(2,1)S(1)}) custom-call(f32[3,3,4096]{2,1,0:T(4,128)} %taps_hbm.3, bf16[3,128,1024]{2,1,0:T(8,128)(2,1)} %br_hbm.3, bf16[128,1024]{1,0:T(8,128)(2,1)} %go_hbm.3, bf16[4,256,256]{2,1,0:T(8,128)(2,1)S(1)} %get-tuple-element.7.corr_ref, ...), custom_call_target="tpu_custom_call" | custom-call | tf_op jit(solution)/shard_map/grad_filter/pallas_call | solution.py:464
  39.9 2.8 %all-to-all-done.1.recv_ref = bf16[32,72,128]{2,1,0:T(8,128)(2,1)S(1)} async-done(((bf16[32,72,128]{2,1,0:T(8,128)(2,1)}), bf16[32,72,128]{2,1,0:T(8,128)(2,1)S(1)}, u32[]{:S(2)}, u32[]{:S(2)}) %all-to-all-start.1) | async-done | bytes 589856 | tf_op jit(solution)/shard_map/all_to_all | solution.py:413
  42.7 1.5 %tail.1 = bf16[3,128,1024]{2,1,0:T(8,128)(2,1)} custom-call(f32[3,3,1024]{2,1,0:T(4,128)S(1)} %get-tuple-element.8.taps_ref, bf16[3,128,1024]{2,1,0:T(8,128)(2,1)S(1)} %get-tuple-element.9.rows_ref, bf16[32,72,128]{2,1,0:T(8,128)(2,1)S(1)} %all-to-all-done.1.recv_ref), custom_call_target="tpu_custom_call" | custom-call | tf_op jit(solution)/shard_map/tail/pallas_call | solution.py:481
Async XLA Ops:
  3.3 13.0 %copy-start.1 = (bf16[512,256]{1,0:T(8,128)(2,1)S(1)}, bf16[512,256]{1,0:T(8,128)(2,1)}, u32[]{:S(2)}) copy-start(bf16[512,256]{1,0:T(8,128)(2,1)} %constant.10.clone.lhs1_ref) | copy-start | bytes 786436
  3.3 13.0 %copy-start.2 = (f32[32,4096]{1,0:T(8,128)S(1)}, f32[32,4096]{1,0:T(8,128)}, u32[]{:S(2)}) copy-start(f32[32,4096]{1,0:T(8,128)} %filter_ref.1) | copy-start | bytes 1572868
  3.3 13.0 %copy-start.4 = (bf16[256,256]{1,0:T(8,128)(2,1)S(1)}, bf16[256,256]{1,0:T(8,128)(2,1)}, u32[]{:S(2)}) copy-start(bf16[256,256]{1,0:T(8,128)(2,1)} %constant.12.clone.fwd_ref) | copy-start | bytes 393220
  3.3 13.0 %copy-start.5 = (f32[2,32,128]{2,1,0:T(8,128)S(1)}, f32[2,32,128]{2,1,0:T(8,128)}, u32[]{:S(2)}) copy-start(f32[2,32,128]{2,1,0:T(8,128)} %constant.14.clone.twist_ref) | copy-start | bytes 98308
  3.3 20.0 %all-to-all-start = ((bf16[32,72,128]{2,1,0:T(8,128)(2,1)}), bf16[32,72,128]{2,1,0:T(8,128)(2,1)S(1)}, u32[]{:S(2)}, u32[]{:S(2)}) async-start(bf16[32,72,128]{2,1,0:T(8,128)(2,1)} %head.1), calls=%async_computation | async-start | bytes 1179648 | tf_op jit(solution)/shard_map/all_to_all | solution.py:413
  16.3 7.0 %copy-start = (bf16[256,512]{1,0:T(8,128)(2,1)S(1)}, bf16[256,512]{1,0:T(8,128)(2,1)}, u32[]{:S(2)}) copy-start(bf16[256,512]{1,0:T(8,128)(2,1)} %constant.11.clone.lhs2_ref) | copy-start | bytes 786436
  16.3 7.0 %copy-start.3 = (bf16[256,256]{1,0:T(8,128)(2,1)S(1)}, bf16[256,256]{1,0:T(8,128)(2,1)}, u32[]{:S(2)}) copy-start(bf16[256,256]{1,0:T(8,128)(2,1)} %constant.13.clone.inv_ref) | copy-start | bytes 393220
  25.8 16.9 %all-to-all-start.1 = ((bf16[32,72,128]{2,1,0:T(8,128)(2,1)}), bf16[32,72,128]{2,1,0:T(8,128)(2,1)S(1)}, u32[]{:S(2)}, u32[]{:S(2)}) async-start(bf16[32,72,128]{2,1,0:T(8,128)(2,1)} %get-tuple-element.10), calls=%async_computation.1 | async-start | bytes 1179648 | tf_op jit(solution)/shard_map/all_to_all | solution.py:413

commit v8 on v6

--- a/solution.py
+++ b/solution.py
@@ -29,7 +29,7 @@
 
 
 ORDER_IN = ctx_order(1)
-ORDER_OUT = ctx_order(-1)
+ORDER_OUT = ctx_order(1)
 PLACE_IN = [ORDER_IN.index(i) for i in range(BLOCKS)]
 PLACE_OUT = [ORDER_OUT.index(i) for i in range(BLOCKS)]
 

time: 44.5 us -> 44.5 us (level)
  no operation moved by 1% of the time
where the time goes in v8:
time: 44.5 us; the launch traced here: 44.2 us
  starting transfers between devices  24.2 us (54%)
  Pallas kernels  9.99 us (22%)
  waiting for transfers between devices  9.16 us (21%)
  between operations  0.76 us (2%)
    all_to_all x2, starting transfers between devices, exchange(): lax.all_to_all(x, 'ctx', split_axis=0, concat_axis=0, axis_index_groups=[...  24.2 us
    all_to_all x2, waiting for transfers between devices, exchange(): lax.all_to_all(x, 'ctx', split_axis=0, concat_axis=0, axis_index_groups=[...  9.16 us
    pallas_call x1, Pallas kernels, per_device(): pl.pallas_call(grad_filter_kernel, in_specs=[hbm, hbm, hbm, vmem, vmem, v...  2.85 us
    pallas_call x1, Pallas kernels, per_device(): pl.pallas_call(head_kernel, in_specs=[hbm, hbm, hbm], out_specs=hbm, out_...  2.64 us
    pallas_call x1, Pallas kernels, per_device(): pl.pallas_call(middle_kernel, in_specs=[vmem] * 7, out_specs=[hbm, vmem],...  2.49 us
    pallas_call x1, Pallas kernels, per_device(): pl.pallas_call(tail_kernel, in_specs=[vmem, vmem, vmem], out_specs=hbm, o...  1.46 us
  transfers between devices with their start and end apart: 2, of which 2 were waited for; matrix products, arithmetic and copies ran while one was open for 0% of the time, Pallas kernels for 8%

profile of v8, /device:TPU:0, one launch (start us, length us, event | category | flops | bytes accessed | tf_op | source)
XLA Modules:
  0.0 44.2 jit_solution(10250351721174753918)
XLA Ops:
  0.6 2.6 %head.1 = bf16[32,72,128]{2,1,0:T(8,128)(2,1)} custom-call(f32[3,3,4096]{2,1,0:T(4,128)} %taps_hbm.3, bf16[3,128,1024]{2,1,0:T(8,128)(2,1)} %br_hbm.3, bf16[128,1024]{1,0:T(8,128)(2,1)} %go_hbm.3), custom_call_target="tpu_custom_call" | custom-call | tf_op jit(solution)/shard_map/head/pallas_call | solution.py:424
  3.3 0.0 copy-start.1
  3.3 0.0 copy-start.2
  3.3 0.0 copy-start.4
  3.3 0.0 copy-start.5
  3.3 13.0 %all-to-all-start = ((bf16[32,72,128]{2,1,0:T(8,128)(2,1)}), bf16[32,72,128]{2,1,0:T(8,128)(2,1)S(1)}, u32[]{:S(2)}, u32[]{:S(2)}) async-start(bf16[32,72,128]{2,1,0:T(8,128)(2,1)} %head.1), calls=%async_computation | async-start | bytes 1179648 | tf_op jit(solution)/shard_map/all_to_all | solution.py:408
  16.3 0.0 copy-done.1
  16.3 0.0 copy-done.2
  16.3 0.0 copy-done.4
  16.3 0.0 copy-done.5
  16.3 0.0 copy-start
  16.4 0.0 copy-start.3
  16.4 0.5 %filter_spectrum.1.spec_ref = bf16[4,256,256]{2,1,0:T(8,128)(2,1)S(1)} custom-call(f32[32,4096]{1,0:T(8,128)S(1)} %copy-done.2, bf16[512,256]{1,0:T(8,128)(2,1)S(1)} %copy-done.1, bf16[256,256]{1,0:T(8,128)(2,1)S(1)} %copy-done.4, f32[2,32,128]{2,1,0:T(8,128)S(1)} %copy-done.5), custom_call_target="tpu_custom_call" | custom-call | tf_op jit(solution)/shard_map/filter_spectrum/pallas_call | solution.py:441
  16.9 6.4 %all-to-all-done.recv_ref = bf16[32,72,128]{2,1,0:T(8,128)(2,1)S(1)} async-done(((bf16[32,72,128]{2,1,0:T(8,128)(2,1)}), bf16[32,72,128]{2,1,0:T(8,128)(2,1)S(1)}, u32[]{:S(2)}, u32[]{:S(2)}) %all-to-all-start) | async-done | bytes 589856 | tf_op jit(solution)/shard_map/all_to_all | solution.py:408
  23.3 0.0 copy-done
  23.3 0.0 copy-done.3
  23.3 2.5 %middle.1 = (bf16[32,72,128]{2,1,0:T(8,128)(2,1)}, bf16[4,256,256]{2,1,0:T(8,128)(2,1)S(1)}) custom-call(bf16[32,72,128]{2,1,0:T(8,128)(2,1)S(1)} %all-to-all-done.recv_ref, bf16[4,256,256]{2,1,0:T(8,128)(2,1)S(1)} %filter_spectrum.1.spec_ref, bf16[512,256]{1,0:T(8,128)(2,1)S(1)} %copy-done.1, bf16[256,512]{1,0:T(8,128)(2,1)S(1)} %copy-done, ...), custom_call_target="tpu_custom_call" | custom-call | tf_op jit(solution)/shard_map/middle/pallas_call | solution.py:450
  25.8 11.3 %all-to-all-start.1 = ((bf16[32,72,128]{2,1,0:T(8,128)(2,1)}), bf16[32,72,128]{2,1,0:T(8,128)(2,1)S(1)}, u32[]{:S(2)}, u32[]{:S(2)}) async-start(bf16[32,72,128]{2,1,0:T(8,128)(2,1)} %get-tuple-element.10), calls=%async_computation.1 | async-start | bytes 1179648 | tf_op jit(solution)/shard_map/all_to_all | solution.py:408
  37.1 2.8 %grad_filter.1 = (f32[32,4096]{1,0:T(8,128)}, f32[3,3,1024]{2,1,0:T(4,128)S(1)}, bf16[3,128,1024]{2,1,0:T(8,128)(2,1)S(1)}) custom-call(f32[3,3,4096]{2,1,0:T(4,128)} %taps_hbm.3, bf16[3,128,1024]{2,1,0:T(8,128)(2,1)} %br_hbm.3, bf16[128,1024]{1,0:T(8,128)(2,1)} %go_hbm.3, bf16[4,256,256]{2,1,0:T(8,128)(2,1)S(1)} %get-tuple-element.7.corr_ref, ...), custom_call_target="tpu_custom_call" | custom-call | tf_op jit(solution)/shard_map/grad_filter/pallas_call | solution.py:459
  39.9 2.8 %all-to-all-done.1.recv_ref = bf16[32,72,128]{2,1,0:T(8,128)(2,1)S(1)} async-done(((bf16[32,72,128]{2,1,0:T(8,128)(2,1)}), bf16[32,72,128]{2,1,0:T(8,128)(2,1)S(1)}, u32[]{:S(2)}, u32[]{:S(2)}) %all-to-all-start.1) | async-done | bytes 589856 | tf_op jit(solution)/shard_map/all_to_all | solution.py:408
  42.7 1.5 %tail.1 = bf16[3,128,1024]{2,1,0:T(8,128)(2,1)} custom-call(f32[3,3,1024]{2,1,0:T(4,128)S(1)} %get-tuple-element.8.taps_ref, bf16[3,128,1024]{2,1,0:T(8,128)(2,1)S(1)} %get-tuple-element.9.rows_ref, bf16[32,72,128]{2,1,0:T(8,128)(2,1)S(1)} %all-to-all-done.1.recv_ref), custom_call_target="tpu_custom_call" | custom-call | tf_op jit(solution)/shard_map/tail/pallas_call | solution.py:476
Async XLA Ops:
  3.3 13.0 %copy-start.1 = (bf16[512,256]{1,0:T(8,128)(2,1)S(1)}, bf16[512,256]{1,0:T(8,128)(2,1)}, u32[]{:S(2)}) copy-start(bf16[512,256]{1,0:T(8,128)(2,1)} %constant.10.clone.lhs1_ref) | copy-start | bytes 786436
  3.3 13.0 %copy-start.2 = (f32[32,4096]{1,0:T(8,128)S(1)}, f32[32,4096]{1,0:T(8,128)}, u32[]{:S(2)}) copy-start(f32[32,4096]{1,0:T(8,128)} %filter_ref.1) | copy-start | bytes 1572868
  3.3 13.0 %copy-start.4 = (bf16[256,256]{1,0:T(8,128)(2,1)S(1)}, bf16[256,256]{1,0:T(8,128)(2,1)}, u32[]{:S(2)}) copy-start(bf16[256,256]{1,0:T(8,128)(2,1)} %constant.12.clone.fwd_ref) | copy-start | bytes 393220
  3.3 13.0 %copy-start.5 = (f32[2,32,128]{2,1,0:T(8,128)S(1)}, f32[2,32,128]{2,1,0:T(8,128)}, u32[]{:S(2)}) copy-start(f32[2,32,128]{2,1,0:T(8,128)} %constant.14.clone.twist_ref) | copy-start | bytes 98308
  3.3 20.0 %all-to-all-start = ((bf16[32,72,128]{2,1,0:T(8,128)(2,1)}), bf16[32,72,128]{2,1,0:T(8,128)(2,1)S(1)}, u32[]{:S(2)}, u32[]{:S(2)}) async-start(bf16[32,72,128]{2,1,0:T(8,128)(2,1)} %head.1), calls=%async_computation | async-start | bytes 1179648 | tf_op jit(solution)/shard_map/all_to_all | solution.py:408
  16.3 7.0 %copy-start = (bf16[256,512]{1,0:T(8,128)(2,1)S(1)}, bf16[256,512]{1,0:T(8,128)(2,1)}, u32[]{:S(2)}) copy-start(bf16[256,512]{1,0:T(8,128)(2,1)} %constant.11.clone.lhs2_ref) | copy-start | bytes 786436
  16.4 7.0 %copy-start.3 = (bf16[256,256]{1,0:T(8,128)(2,1)S(1)}, bf16[256,256]{1,0:T(8,128)(2,1)}, u32[]{:S(2)}) copy-start(bf16[256,256]{1,0:T(8,128)(2,1)} %constant.13.clone.inv_ref) | copy-start | bytes 393220
  25.8 16.9 %all-to-all-start.1 = ((bf16[32,72,128]{2,1,0:T(8,128)(2,1)}), bf16[32,72,128]{2,1,0:T(8,128)(2,1)S(1)}, u32[]{:S(2)}, u32[]{:S(2)}) async-start(bf16[32,72,128]{2,1,0:T(8,128)(2,1)} %get-tuple-element.10), calls=%async_computation.1 | async-start | bytes 1179648 | tf_op jit(solution)/shard_map/all_to_all | solution.py:408
